TPU v7x, 128 devices: a whole 4x4x4 slice. The times are simulated.
128 devices in a mesh: rep: 16 (over y, z_hi, core), tp: 8 (over x, z_lo).
Axes of the slice: x: 4, y: 4, z: 4 (z_hi: 2, z_lo: 2; z = z_hi * 2 + z_lo), core: 2. Of those that a mesh axis runs over, the one named last changes fastest.
Arguments:
- inputs: bfloat16 [4, 1024, 5120], P(None, 'rep'), may hold values from -6 to 6
- qkv_weight: bfloat16 [2, 5120, 6144], P(None, ('rep', 'tp')), may hold values from -0.078125 to 0.078125
- out_weight: bfloat16 [2, 5120, 4096], P(None, ('rep', 'tp')), may hold values from -0.25 to 0.25
- norm_gain: float32 [2, 5120], replicated, may hold values from 0.1 to 1.9
- query_gain: float32 [2, 128], replicated, may hold values from 0.5 to 2
- key_gain: float32 [2, 128], replicated, may hold values from 0.5 to 2
- stored_rotated_keys: bfloat16 [2, 1024, 8, 256, 128], P(None, 'rep', 'tp'), may hold values from -540 to 540
- stored_cache_values: bfloat16 [2, 1024, 8, 256, 128], P(None, 'rep', 'tp'), may hold values from -6 to 6
- lengths: int32 [1024], P('rep'), may hold values from 1 to 256, as said below
Outputs:
- final_hidden: bfloat16 [4, 1024, 5120], P(None, 'rep')
Inputs may be any that keep to these rules, and one draw needn't show every extreme that they name: `lengths`: in every replica some row has exactly 256 cached positions.
All inputs are finite; a program needn't handle non-finite values.
Results may differ from a plain program's by a relative error of at most 0.039.
The roundings to bfloat16 on the way count: a program that leaves them out, or rounds other values in their place, can miss the bound.
Values may be sent and summed in bfloat16 or wider, within the bound.
A program may use at most 192 MiB of HBM per device.

v0:
```python
import jax
import jax.numpy as jnp
from jax import lax
from jax.sharding import PartitionSpec as P

epsilon = 1e-06
rope_base = 1000000.0


def rms_scale(value_rows, gain):
    wide = value_rows.astype(jnp.float32)
    return wide * lax.rsqrt(jnp.mean(wide * wide, axis=-1, keepdims=True) + epsilon) * gain


def rotate(value_rows, positions):
    half_dim = value_rows.shape[-1] // 2
    frequency = rope_base ** (-jnp.arange(half_dim, dtype=jnp.float32) / half_dim)
    angles = positions.astype(jnp.float32)[..., None] * frequency
    cosine = jnp.cos(angles)
    sine = jnp.sin(angles)
    leading_shape = value_rows[..., :half_dim]
    trailing_shape = value_rows[..., half_dim:]
    return jnp.concatenate(
        [
            leading_shape * cosine - trailing_shape * sine,
            trailing_shape * cosine + leading_shape * sine,
        ],
        axis=-1,
    )


def attend(queries, new_keys, new_values, old_keys, old_values, lengths):
    step_count = queries.shape[0]
    head_dim = queries.shape[-1]
    slots = old_keys.shape[2]
    score_old = jnp.einsum(
        "srkgd,rkcd->srkgc", queries, old_keys, preferred_element_type=jnp.float32
    ) * head_dim ** (-0.5)
    score_new = jnp.einsum(
        "srkgd,trkd->srkgt", queries, new_keys, preferred_element_type=jnp.float32
    ) * head_dim ** (-0.5)
    live = jnp.arange(slots, dtype=jnp.int32)[None, :] < lengths[:, None]
    score_old = jnp.where(live[None, :, None, None, :], score_old, -jnp.inf)
    order = jnp.arange(step_count, dtype=jnp.int32)
    causal = order[None, :] <= order[:, None]
    score_new = jnp.where(causal[:, None, None, None, :], score_new, -jnp.inf)
    highest = jnp.maximum(jnp.max(score_old, axis=-1), jnp.max(score_new, axis=-1))[..., None]
    weight_old = jnp.exp(score_old - highest)
    weight_new = jnp.exp(score_new - highest)
    denominator = jnp.sum(weight_old, axis=-1, keepdims=True) + jnp.sum(
        weight_new, axis=-1, keepdims=True
    )
    share_old = (weight_old / denominator).astype(jnp.bfloat16)
    share_new = (weight_new / denominator).astype(jnp.bfloat16)
    mixed = jnp.einsum(
        "srkgc,rkcd->srkgd", share_old, old_values, preferred_element_type=jnp.float32
    )
    mixed = mixed + jnp.einsum(
        "srkgt,trkd->srkgd", share_new, new_values, preferred_element_type=jnp.float32
    )
    return mixed.astype(jnp.bfloat16)


def on_device(
    inputs,
    qkv_weight,
    out_weight,
    norm_gain,
    query_gain,
    key_gain,
    stored_rotated_keys,
    stored_cache_values,
    lengths,
):
    step_count = inputs.shape[0]
    row_count = inputs.shape[1]
    model_width = inputs.shape[2]
    flat_rows = step_count * row_count
    groups_here = stored_rotated_keys.shape[2]
    head_dim = stored_rotated_keys.shape[4]
    per_group = qkv_weight.shape[2] // (lax.axis_size("tp") * groups_here * head_dim)
    block_qkv, block_out = (
        lax.all_to_all(qkv_weight, "tp", split_axis=2, concat_axis=1, tiled=True),
        lax.all_to_all(out_weight, "tp", split_axis=2, concat_axis=1, tiled=True),
    )
    rows_qkv, rows_out = (
        lax.all_gather(block_qkv, "rep", axis=1, tiled=True),
        lax.all_gather(block_out, "rep", axis=1, tiled=True),
    )
    positions = lengths[None, :] + jnp.arange(step_count, dtype=jnp.int32)[:, None]
    hidden = inputs
    for layer_index in range(qkv_weight.shape[0]):
        normed = (
            rms_scale(hidden, norm_gain[layer_index])
            .astype(jnp.bfloat16)
            .reshape(flat_rows, model_width)
        )
        mixed = jnp.dot(normed, rows_qkv[layer_index], preferred_element_type=jnp.float32)
        mixed = mixed.reshape(step_count, row_count, groups_here, per_group, head_dim)
        queries = rotate(
            rms_scale(mixed[:, :, :, : per_group - 2], query_gain[layer_index]),
            positions[:, :, None, None],
        ).astype(jnp.bfloat16)
        new_keys = rotate(
            rms_scale(mixed[:, :, :, per_group - 2], key_gain[layer_index]), positions[:, :, None]
        ).astype(jnp.bfloat16)
        new_values = mixed[:, :, :, per_group - 1].astype(jnp.bfloat16)
        attended = attend(
            queries,
            new_keys,
            new_values,
            stored_rotated_keys[layer_index],
            stored_cache_values[layer_index],
            lengths,
        )
        attended = attended.reshape(flat_rows, -1)
        projected = lax.dot_general(
            attended,
            rows_out[layer_index],
            (((1,), (1,)), ((), ())),
            preferred_element_type=jnp.float32,
        )
        summed = lax.psum(projected, "tp")
        hidden = (
            hidden.astype(jnp.float32) + summed.reshape(step_count, row_count, model_width)
        ).astype(jnp.bfloat16)
    return hidden


def solution(mesh):
    return jax.shard_map(
        on_device,
        mesh=mesh,
        in_specs=(
            P(None, "rep", None),
            P(None, ("rep", "tp"), None),
            P(None, ("rep", "tp"), None),
            P(),
            P(),
            P(),
            P(None, "rep", "tp", None, None),
            P(None, "rep", "tp", None, None),
            P("rep"),
        ),
        out_specs=P(None, "rep", None),
        check_vma=False,
    )
```

profile of v0, /device:TPU:32, one launch (start us, length us, event | category | flops | bytes accessed | tf_op | source)
XLA Modules:
  0.0 725.6 jit_solution(6297289012049457406)
XLA Ops:
  6.5 6.7 copy.69
  13.2 5.8 reshape.509
  19.0 19.8 %all_to_all.36 = bf16[8,2,30720]{2,1,0:T(2,128)(2,1)} all-to-all(bf16[8,2,30720]{2,1,0:T(2,128)(2,1)} %reshape.509), channel_id=1, replica_groups=mesh['rep'=16,'tp'=8] {'tp'}, dimensions={0} | all-to-all | bytes 1966080 | tf_op jit(solution)/shard_map/all_to_all | solution.py:83
  38.8 5.7 reshape.510
  44.5 5.0 copy.109
  49.5 0.0 all-gather.3.cloned.1.call-update
  49.6 0.0 all-gather.5.cloned.1.call-start
  49.6 5.4 copy.82
  55.0 8.3 %reshape.507 = bf16[8,2,20480]{2,1,0:T(2,128)(2,1)S(1)} reshape(bf16[4096,2,40]{2,1,0:T(2,128)(2,1)} %bitcast.261) | data formatting | bytes 1310720
  63.3 13.5 %all_to_all.37 = bf16[8,2,20480]{2,1,0:T(2,128)(2,1)} all-to-all(bf16[8,2,20480]{2,1,0:T(2,128)(2,1)S(1)} %reshape.507), channel_id=1, replica_groups=mesh['rep'=16,'tp'=8] {'tp'}, dimensions={0} | all-to-all | bytes 1310720 | tf_op jit(solution)/shard_map/all_to_all | solution.py:84
  76.8 9.3 %reshape.508 = bf16[4096,2,40]{2,1,0:T(2,128)(2,1)} reshape(bf16[8,2,20480]{2,1,0:T(2,128)(2,1)} %all_to_all.37) | data formatting | bytes 1310720
  86.1 5.8 copy.115
  91.9 0.2 all-reduce.3.cloned.1.call-start
  92.2 0.6 fusion
  92.8 0.1 iota_compare_fusion
  92.9 0.5 multiply_cosine_fusion.1
  93.5 68.7 %all-gather.3.cloned.1.call-done = bf16[2,5120,768]{2,1,0:T(8,128)(2,1)} async-done(((bf16[2,320,768]{2,1,0:T(8,128)(2,1)}), bf16[2,5120,768]{2,1,0:T(8,128)(2,1)}) %all-gather.3.cloned.1.call-update) | async-done | bytes 15728656 | tf_op jit(solution)/shard_map/all_gather | solution.py:87
  162.2 11.0 %slice_bitcast_fusion.1 = (bf16[768,5120]{0,1:T(8,128)(2,1)}, bf16[768,5120]{0,1:T(8,128)(2,1)}) fusion(bf16[2,5120,768]{2,1,0:T(8,128)(2,1)} %all-gather.3.cloned.1.call-done), kind=kLoop, calls=%fused_computation.1 | loop fusion | bytes 31457280 | tf_op jit(solution)/shard_map/dot_general | solution.py:98
  173.2 10.6 %copy.72 = bf16[768,5120]{1,0:T(8,128)(2,1)} copy(bf16[768,5120]{0,1:T(8,128)(2,1)} %get-tuple-element.7) | data formatting | bytes 15728640 | tf_op jit(solution)/shard_map/dot_general | solution.py:98
  183.8 5.5 fusion.28
  189.3 0.1 multiply_reduce_fusion.3
  189.4 0.1 multiply_multiply_fusion.3
  189.5 0.6 fusion.99
  190.1 0.1 maximum_bitcast_fusion
  190.2 0.2 multiply_reduce_fusion.1
  190.5 0.2 multiply_multiply_fusion.1
  190.7 0.3 fusion.58
  190.9 0.2 pad_maximum_fusion
  191.1 2.5 fusion.103
  193.7 1.3 fusion.102
  195.1 0.5 fusion.56
  195.5 0.8 fusion.50
  196.4 0.5 fusion.68
  196.9 1.2 fusion.42
  198.1 0.1 copy.81
  198.2 45.6 %all-gather.5.cloned.1.call-done = bf16[2,5120,512]{2,1,0:T(8,128)(2,1)} async-done(((bf16[2,320,512]{2,1,0:T(8,128)(2,1)}), bf16[2,5120,512]{2,1,0:T(8,128)(2,1)}) %all-gather.5.cloned.1.call-update) | async-done | bytes 10485776 | tf_op jit(solution)/shard_map/all_gather | solution.py:88
  243.8 6.4 fusion.9
  250.2 0.3 all-reduce.5.cloned.1.call-start
  250.5 10.5 %copy.85 = bf16[768,5120]{1,0:T(8,128)(2,1)} copy(bf16[768,5120]{0,1:T(8,128)(2,1)} %get-tuple-element.8) | data formatting | bytes 15728640 | tf_op jit(solution)/shard_map/dot_general | solution.py:98
  261.0 207.9 %all-reduce.3.cloned.1.call-done = f32[4,64,5120]{2,1,0:T(8,128)} async-done(((f32[4,64,5120]{2,1,0:T(8,128)}), f32[4,64,5120]{2,1,0:T(8,128)}) %all-reduce.3.cloned.1.call-update) | async-done | bytes 5242896 | tf_op jit(solution)/shard_map/psum | solution.py:123
  468.9 4.5 fusion.4
  473.4 1.0 copy-done.1
  474.4 2.3 fusion.31
  476.7 0.2 multiply_reduce_fusion
  477.0 0.1 multiply_reduce_fusion.2
  477.1 0.2 multiply_multiply_fusion
  477.3 0.3 fusion.60
  477.6 0.2 pad_maximum_fusion.1
  477.8 1.3 fusion.104
  479.1 0.1 multiply_multiply_fusion.2
  479.2 0.6 fusion.97
  479.8 0.1 maximum_bitcast_fusion.1
  479.9 2.5 fusion.105
  482.5 0.5 fusion.57
  483.0 0.8 fusion.51
  483.9 0.5 fusion.66
  484.4 1.2 fusion.43
  485.6 0.1 copy.94
  485.7 0.3 slice-done
  486.0 1.4 slice-done.1
  487.5 0.6 slice-done.2
  488.1 3.9 fusion.8
  492.0 222.4 %all-reduce.5.cloned.1.call-done = f32[4,64,5120]{2,1,0:T(8,128)} async-done(((f32[4,64,5120]{2,1,0:T(8,128)}), f32[4,64,5120]{2,1,0:T(8,128)}) %all-reduce.5.cloned.1.call-update) | async-done | bytes 5242896 | tf_op jit(solution)/shard_map/psum | solution.py:123
  714.4 4.7 fusion.7
  (57 shorter events, 0.4 us)
Async XLA Ops:
  6.5 155.6 %all-gather.3.cloned.1.call-start = ((), (), s32[]{:S(2)}) async-start(), calls=%async_computation.2 | async-start | bytes 16711680 | tf_op jit(solution)/shard_map/all_gather | solution.py:87
  49.6 194.3 %all-gather.5.cloned.1.call-start = ((), (), s32[]{:S(2)}) async-start(), calls=%async_computation.3 | async-start | bytes 11141120 | tf_op jit(solution)/shard_map/all_gather | solution.py:88
  55.0 37.1 %copy-start.4 = (f32[2,128]{1,0:T(2,128)S(1)}, f32[2,128]{1,0:T(2,128)}, u32[]{:S(2)}) copy-start(f32[2,128]{1,0:T(2,128)} %param.13) | copy-start | bytes 3076
  55.0 37.2 %copy-start.5 = (f32[2,128]{1,0:T(2,128)S(1)}, f32[2,128]{1,0:T(2,128)}, u32[]{:S(2)}) copy-start(f32[2,128]{1,0:T(2,128)} %param.14) | copy-start | bytes 3076
  55.0 37.2 %copy-start.3 = (s32[64]{0:T(128)S(1)}, s32[64]{0:T(128)}, u32[]{:S(2)}) copy-start(s32[64]{0:T(128)} %param.17) | copy-start | bytes 772
  55.0 37.2 %copy-start = (bf16[4,64,5120]{2,1,0:T(8,128)(2,1)S(1)}, bf16[4,64,5120]{2,1,0:T(8,128)(2,1)}, u32[]{:S(2)}) copy-start(bf16[4,64,5120]{2,1,0:T(8,128)(2,1)} %param.9) | copy-start | bytes 7864324
  63.3 30.2 %copy-start.2 = (f32[2,5120]{1,0:T(2,128)S(1)}, f32[2,5120]{1,0:T(2,128)}, u32[]{:S(2)}) copy-start(f32[2,5120]{1,0:T(2,128)} %param.12) | copy-start | bytes 122884
  91.9 377.0 %all-reduce.3.cloned.1.call-start = ((), (), s32[]{:S(2)}) async-start(), calls=%async_computation.4 | async-start | bytes 10485760 | tf_op jit(solution)/shard_map/psum | solution.py:123
  183.8 9.8 %slice-start.3 = ((s8[8388608]{0:T(1024)(128)(4,1)}), s8[4194304]{0:T(1024)(128)(4,1)S(1)}, s32[]{:S(2)}) async-start(s8[8388608]{0:T(1024)(128)(4,1)} %bitcast.270), calls=%async_computation.9 | async-start | bytes 8388608
  183.8 9.8 %slice-start.4 = ((s8[8388608]{0:T(1024)(128)(4,1)}), s8[4194304]{0:T(1024)(128)(4,1)S(1)}, s32[]{:S(2)}) async-start(s8[8388608]{0:T(1024)(128)(4,1)} %bitcast.270), calls=%async_computation.10 | async-start | bytes 8388608
  191.1 5.8 slice-start.7
  193.7 3.3 slice-start.8
  250.2 464.2 %all-reduce.5.cloned.1.call-start = ((), (), s32[]{:S(2)}) async-start(), calls=%async_computation.5 | async-start | bytes 10485760 | tf_op jit(solution)/shard_map/psum | solution.py:123
  468.9 5.5 copy-start.1
  468.9 8.9 %slice-start.5 = ((s8[8388608]{0:T(1024)(128)(4,1)}), s8[4194304]{0:T(1024)(128)(4,1)S(1)}, s32[]{:S(2)}) async-start(s8[8388608]{0:T(1024)(128)(4,1)} %bitcast.273), calls=%async_computation.11 | async-start | bytes 8388608
  474.4 3.3 slice-start.6
  477.8 6.6 slice-start.9
  479.9 4.4 slice-start.10
  483.9 2.2 slice-start
  484.4 3.1 slice-start.1
  484.4 3.7 slice-start.2
Sparse Core Ops, SparseCore 0:
  49.7 112.4 all-gather.2
  164.6 79.1 all-gather.4
  250.3 218.5 all-reduce.2
  492.1 222.2 all-reduce.4
where the time goes:
time: 730 us; the launch traced here: 726 us
  waiting for transfers between devices  545 us (75%)
  local copies, waits for them, and re-layouts  87.8 us (12%)
  blocking collectives  33.3 us (5%)
  matrix products  29.1 us (4%)
  other arithmetic  16.7 us (2%)
  between operations  13.6 us (2%)
    psum x2, waiting for transfers between devices, on_device(): summed = lax.psum(projected, 'tp')  430 us
    all_gather x1, waiting for transfers between devices, on_device(): lax.all_gather(block_qkv, 'rep', axis=1, tiled=True)  68.7 us
    all_gather x1, waiting for transfers between devices, on_device(): lax.all_gather(block_out, 'rep', axis=1, tiled=True)  45.6 us
    unnamed x40, local copies, waits for them, and re-layouts  44.5 us
    dot_general x3, local copies, waits for them, and re-layouts, on_device(): jnp.dot(normed, rows_qkv[layer_index], preferred_element_type=jnp.float32)  32.2 us
    all_to_all x1, blocking collectives, on_device(): lax.all_to_all(qkv_weight, 'tp', split_axis=2, concat_axis=1, tiled=True)  19.8 us
  transfers between devices with their start and end apart: 4, of which 4 were waited for; matrix products, arithmetic and copies ran while one was open for 11% of the time, Pallas kernels for 0%

commit v1 on v0

v1 whole, which is shorter than its diff:
```python
import functools

import jax
import jax.numpy as jnp
from jax import lax
from jax.experimental import pallas as pl
from jax.experimental.pallas import tpu as pltpu
from jax.sharding import PartitionSpec as P

MESH = pl.DeviceIdType.MESH
epsilon = 1e-06
rope_base = 1000000.0

LAYERS = 2
STEPS = 4
ROWS = 64
FLAT = STEPS * ROWS
D = 5120
CHUNKS = 8
CHUNK = D // CHUNKS
OWN = 40
PAD = 48
HEAD = 128
GROUP = 768
ATT = 512
SLOTS = 256
HALF = 2048
TP = 8
f32 = jnp.float32
bf16 = jnp.bfloat16

NT = (((1,), (1,)), ((), ()))


def kernel(
    x_hbm, qw, ow, resid, gain, qgain, kgain, cosf, sinf, len16, k_hbm, v_hbm,
    out,
    wq, wo, land_q, land_o, pack, xin, norm, hid, hown, att, kbuf, vbuf, qs, ao, nk, nv, mixed,
    a2a_s, a2a_r, ex_s, ex_r, q_s, q_r, o_s, o_r, g_s, g_r, loc,
):
    r = lax.axis_index("rep")
    t = lax.axis_index("tp")
    y = lax.div(r, 4)
    zh = lax.rem(lax.div(r, 2), 2)
    c = lax.rem(r, 2)
    p = lax.div(r, 2)
    x = lax.div(t, 2)
    zl = lax.rem(t, 2)

    def rep(y_, zh_, c_):
        return y_ * 4 + zh_ * 2 + c_

    yp, ym, y2 = lax.rem(y + 1, 4), lax.rem(y + 3, 4), lax.rem(y + 2, 4)
    xp, xm = lax.rem(x + 1, 4), lax.rem(x + 3, 4)
    dev_yp = (rep(yp, zh, c), t)
    dev_ym = (rep(ym, zh, c), t)
    dev_z = (rep(y, 1 - zh, c), t)
    dev_sib = (rep(y, zh, 1 - c), t)
    dev_xp = (r, xp * 2 + zl)
    dev_xm = (r, xm * 2 + zl)
    dev_zl = (r, x * 2 + 1 - zl)

    sent = []

    def send(src, dst, ss, rs, dev):
        copy = pltpu.make_async_remote_copy(
            src_ref=src, dst_ref=dst, send_sem=ss, recv_sem=rs, device_id=dev, device_id_type=MESH
        )
        copy.start()
        sent.append(copy)

    def got(ref, rs):
        pltpu.make_async_remote_copy(
            src_ref=ref, dst_ref=ref, send_sem=rs, recv_sem=rs, device_id=dev_sib, device_id_type=MESH
        ).wait_recv()

    barrier = pltpu.get_barrier_semaphore()
    greet = [dev_yp, dev_ym, dev_z, dev_sib]
    for k in range(1, TP):
        other = lax.rem(t + k, TP)
        greet.append((r, other))
        greet.append((rep(y, zh, 1 - c), other))
    for dev in greet:
        pl.semaphore_signal(barrier, inc=1, device_id=dev, device_id_type=MESH)
    pl.semaphore_wait(barrier, len(greet))

    load_x = pltpu.make_async_copy(x_hbm, xin, loc.at[0])
    load_x.start()
    kv = {}

    def load_kv(layer):
        kv[layer] = [
            pltpu.make_async_copy(k_hbm.at[layer], kbuf, loc.at[1]),
            pltpu.make_async_copy(v_hbm.at[layer], vbuf, loc.at[2]),
        ]
        for copy in kv[layer]:
            copy.start()

    def qcols(other):
        return pl.ds(pl.multiple_of(other * GROUP, GROUP), GROUP)

    half_of_t = lax.div(t, 4)
    slot1 = lax.rem(t, 4) * 2 + c
    for k in range(1, TP):
        other = lax.rem(t + k, TP)
        send(qw.at[0, :, qcols(other)], land_q.at[0, t], a2a_s.at[0, k], a2a_r.at[0, t], (r, other))
    own0 = pltpu.make_async_copy(qw.at[0, :, qcols(t)], land_q.at[0, t], a2a_r.at[0, t])
    own0.start()
    load_kv(0)

    def start_exchange():
        for layer in range(LAYERS):
            theirs = pl.ds(pl.multiple_of((1 - c) * HALF, HALF), HALF)
            mine = pl.ds(pl.multiple_of(c * HALF, HALF), HALF)
            send(ow.at[layer, :, theirs], land_o.at[layer, c], ex_s.at[layer], ex_r.at[layer, c], dev_sib)
            pltpu.make_async_copy(ow.at[layer, :, mine], land_o.at[layer, c], ex_r.at[layer, 2]).start()

    def sibling_slab():
        return pltpu.make_async_remote_copy(
            src_ref=qw.at[1, :, qcols(t)], dst_ref=land_q.at[1, slot1], send_sem=a2a_s.at[1, 0],
            recv_sem=a2a_r.at[1, slot1], device_id=dev_sib, device_id_type=MESH,
        )

    def start_second():
        for k in range(1, TP):
            other = lax.rem(t + k, TP)
            send(
                qw.at[1, :, qcols(other)], land_q.at[1, slot1], a2a_s.at[1, k], a2a_r.at[1, slot1],
                (rep(y, zh, half_of_t), other),
            )

        @pl.when(half_of_t == c)
        def _():
            pltpu.make_async_copy(qw.at[1, :, qcols(t)], land_q.at[1, slot1], a2a_r.at[1, slot1]).start()

        @pl.when(half_of_t != c)
        def _():
            sibling_slab().start()

    def pack_q(layer):
        for slot in range(TP):
            got(land_q.at[layer, slot], a2a_r.at[layer, slot])
        for slot in range(TP):
            pack[slot * OWN : (slot + 1) * OWN, :] = land_q[layer, slot].astype(f32)[:OWN]
        if layer == 0:
            wq[0, p, pl.ds(pl.multiple_of(c * 320, 320), 320), :] = pack[...].astype(bf16)
        else:
            for k in range(4):
                wq[1, 4 * c + k, pl.ds(pl.multiple_of(p * 80, 80), 80), :] = pack[k * 80 : (k + 1) * 80, :].astype(bf16)

    def pack_o(layer):
        pltpu.make_async_copy(ow.at[layer, :, pl.ds(0, HALF)], land_o.at[layer, c], ex_r.at[layer, 2]).wait()
        got(land_o.at[layer, 1 - c], ex_r.at[layer, 1 - c])
        for cut in range(4):
            cols = slice(cut * 512, (cut + 1) * 512)
            both = jnp.concatenate(
                [land_o[layer, core, :, cols].astype(f32)[:OWN] for core in range(2)], axis=0
            )
            wo[layer, c, pl.ds(pl.multiple_of(p * 80, 80), 80), cols] = both.astype(bf16)

    def qblk(layer, y_, zh_, core):
        if layer == 0:
            return wq.at[0, y_ * 2 + zh_, pl.ds(pl.multiple_of(core * 320, 320), 320), :]
        return wq.at[1, pl.ds(4 * core, 4), pl.ds(pl.multiple_of((y_ * 2 + zh_) * 80, 80), 80), :]

    ring_y = [y, yp, y2, ym]

    def zsel(e):
        return zh if e == 0 else 1 - zh

    def q_send(layer, d, e, dev, idx):
        b = qblk(layer, ring_y[d], zsel(e), c)
        send(b, b, q_s.at[layer, idx], q_r.at[layer, idx], dev)

    def q_got(layer, d, e, idx):
        got(qblk(layer, ring_y[d], zsel(e), c), q_r.at[layer, idx])

    def q_sib(layer, d, e):
        q_send(layer, d, e, dev_sib, 7 + d * 2 + e)

    def q1(layer):
        q_send(layer, 0, 0, dev_z, 0)
        q_send(layer, 0, 0, dev_yp, 1)
        q_send(layer, 0, 0, dev_ym, 3)
        q_sib(layer, 0, 0)

    def q2(layer):
        q_got(layer, 0, 1, 0)
        q_send(layer, 0, 1, dev_yp, 2)
        q_send(layer, 0, 1, dev_ym, 4)
        q_sib(layer, 0, 1)

    def q3(layer):
        q_got(layer, 3, 0, 1)
        q_send(layer, 3, 0, dev_yp, 5)
        q_sib(layer, 3, 0)
        q_got(layer, 1, 0, 3)
        q_sib(layer, 1, 0)
        q_got(layer, 1, 1, 4)
        q_send(layer, 1, 1, dev_ym, 6)
        q_sib(layer, 1, 1)
        q_got(layer, 3, 1, 2)
        q_sib(layer, 3, 1)

    def q4(layer):
        q_got(layer, 2, 0, 5)
        q_sib(layer, 2, 0)
        q_got(layer, 2, 1, 6)
        q_sib(layer, 2, 1)

    def q5(layer):
        for d in range(4):
            for e in range(2):
                got(qblk(layer, ring_y[d], zsel(e), 1 - c), q_r.at[layer, 7 + d * 2 + e])

    def oblk(layer, y_, zh_, core, part=None):
        cols = slice(None) if part is None else pl.ds(part * 1024, 1024)
        return wo.at[layer, core, pl.ds(pl.multiple_of((y_ * 2 + zh_) * 80, 80), 80), cols]

    def o_send(layer, d, e, dev, idx, part=None):
        b = oblk(layer, ring_y[d], zsel(e), c, part)
        send(b, b, o_s.at[layer, idx], o_r.at[layer, idx], dev)

    def o_got(layer, d, e, idx, part=None):
        got(oblk(layer, ring_y[d], zsel(e), c, part), o_r.at[layer, idx])

    def o_pass(layer, d):
        o_send(layer, d, 0, dev_z, 4 + d)
        o_send(layer, d, 0, dev_sib, 8 + d * 2)

    def o1(layer):
        o_send(layer, 0, 0, dev_yp, 0)
        o_send(layer, 0, 0, dev_ym, 1)
        o_pass(layer, 0)

    def o2(layer):
        o_got(layer, 3, 0, 0)
        o_send(layer, 3, 0, dev_yp, 2, 0)
        o_pass(layer, 3)
        o_got(layer, 1, 0, 1)
        o_send(layer, 1, 0, dev_ym, 3, 1)
        o_pass(layer, 1)

    def o3(layer):
        o_got(layer, 2, 0, 2, 0)
        o_got(layer, 2, 0, 3, 1)
        o_pass(layer, 2)

    def o4(layer):
        for d in (0, 3, 1, 2):
            o_got(layer, d, 1, 4 + d)
            o_send(layer, d, 1, dev_sib, 8 + d * 2 + 1)

    def o5(layer):
        for d in range(4):
            for e in range(2):
                got(oblk(layer, ring_y[d], zsel(e), 1 - c), o_r.at[layer, 8 + d * 2 + e])

    ring_x = [x, xp, lax.rem(x + 2, 4), xm]

    def tsel(d, e):
        return ring_x[d] * 2 + (zl if e == 0 else 1 - zl)

    def g_send(n, ref, d, e, dev, idx, own=None):
        b = ref(tsel(d, e))
        send(b if own is None else own, b, g_s.at[n, idx], g_r.at[n, idx], dev)

    def g_got(n, ref, d, e, idx):
        got(ref(tsel(d, e)), g_r.at[n, idx])

    def g1(n, ref, own=None):
        g_send(n, ref, 0, 0, dev_zl, 0, own)
        g_send(n, ref, 0, 0, dev_xp, 1, own)
        g_send(n, ref, 0, 0, dev_xm, 3, own)

    def g2(n, ref):
        g_got(n, ref, 0, 1, 0)
        g_send(n, ref, 0, 1, dev_xp, 2)
        g_send(n, ref, 0, 1, dev_xm, 4)

    def g3(n, ref):
        g_got(n, ref, 3, 0, 1)
        g_send(n, ref, 3, 0, dev_xp, 5)
        g_got(n, ref, 1, 0, 3)
        g_got(n, ref, 1, 1, 4)
        g_send(n, ref, 1, 1, dev_xm, 6)
        g_got(n, ref, 3, 1, 2)

    def g4(n, ref):
        g_got(n, ref, 2, 0, 5)
        g_got(n, ref, 2, 1, 6)

    def normalize(layer, read):
        def body(b, carry):
            rows = pl.ds(pl.multiple_of(b * 32, 32), 32)
            total = jnp.zeros((32, 1), f32)
            for j in range(CHUNKS):
                wide = read(rows, j).astype(f32)
                total = total + jnp.sum(wide * wide, axis=-1, keepdims=True)
            scale = lax.rsqrt(total * (1.0 / D) + epsilon)
            for j in range(CHUNKS):
                norm[j, rows, :] = (read(rows, j).astype(f32) * scale * gain[layer, j]).astype(bf16)
            return carry

        lax.fori_loop(0, FLAT // 32, body, 0)

    def project_in(layer):
        mixed[...] = jnp.zeros_like(mixed)

        def body(j, carry):
            mixed[...] += jnp.dot(norm[j], wq[layer, j], preferred_element_type=f32)
            return carry

        lax.fori_loop(0, CHUNKS, body, 0)

        def turn(v, g):
            n = v * lax.rsqrt(jnp.mean(v * v, axis=-1, keepdims=True) + epsilon) * g
            return n * cosf[...] + pltpu.roll(n, HEAD // 2, 1) * sinf[...]

        for i in range(4):
            q = turn(mixed[:, i * HEAD : (i + 1) * HEAD], qgain[layer])
            for s in range(STEPS):
                qs[(s * 4 + i) * ROWS : (s * 4 + i + 1) * ROWS, :] = q[s * ROWS : (s + 1) * ROWS]
        nk[...] = turn(mixed[:, 4 * HEAD : 5 * HEAD], kgain[layer])
        nv[...] = mixed[:, 5 * HEAD : 6 * HEAD]

    row = lax.broadcasted_iota(jnp.int32, (128, 32), 0)
    col = lax.broadcasted_iota(jnp.int32, (128, 32), 1)
    fresh = jnp.logical_and(
        jnp.right_shift(row, 4) == jnp.bitwise_and(col, 7),
        jnp.right_shift(col, 3) <= jnp.bitwise_and(jnp.right_shift(row, 2), 3),
    )
    slot_index = lax.broadcasted_iota(jnp.int32, (128, SLOTS), 1)

    def attend(layer):
        for copy in kv[layer]:
            copy.wait()

        def body(g, carry):
            q = [qs[pl.ds(g * 8 + k, 16, stride=ROWS), :].astype(bf16) for k in range(8)]
            old = jnp.concatenate(
                [lax.dot_general(q[k], kbuf[g * 8 + k], NT, preferred_element_type=f32) for k in range(8)], axis=0
            ) * HEAD ** (-0.5)
            part = [pl.ds(pl.multiple_of(s * ROWS + g * 8, 8), 8) for s in range(STEPS)]
            keys = jnp.concatenate([nk[w, :] for w in part], axis=0).astype(bf16)
            values = jnp.concatenate([nv[w, :] for w in part], axis=0).astype(bf16)
            new = lax.dot_general(jnp.concatenate(q, axis=0), keys, NT, preferred_element_type=f32) * HEAD ** (-0.5)
            live = slot_index < len16[pl.ds(pl.multiple_of(g * 128, 128), 128), :]
            old = jnp.where(live, old, -jnp.inf)
            new = jnp.where(fresh, new, -jnp.inf)
            top = jnp.maximum(jnp.max(old, axis=-1, keepdims=True), jnp.max(new, axis=-1, keepdims=True))
            old = jnp.exp(old - top)
            new = jnp.exp(new - top)
            below = jnp.sum(old, axis=-1, keepdims=True) + jnp.sum(new, axis=-1, keepdims=True)
            old = (old / below).astype(bf16)
            new = (new / below).astype(bf16)
            fresh_part = jnp.dot(new, values, preferred_element_type=f32)
            for k in range(8):
                rows = slice(k * 16, (k + 1) * 16)
                ao[pl.ds(g * 8 + k, 16, stride=ROWS), :] = (
                    jnp.dot(old[rows], vbuf[g * 8 + k], preferred_element_type=f32) + fresh_part[rows]
                )
            return carry

        lax.fori_loop(0, ROWS // 8, body, 0)
        for s in range(STEPS):
            for i in range(4):
                att[layer, t, s * ROWS : (s + 1) * ROWS, i * HEAD : (i + 1) * HEAD] = ao[
                    (s * 4 + i) * ROWS : (s * 4 + i + 1) * ROWS, :
                ].astype(bf16)

    def project_out(layer, before):
        total = before.astype(f32)
        part = jnp.zeros((FLAT, CHUNK), f32)
        for k in range(TP):
            part = part + lax.dot_general(
                att[layer, k], wo[layer, k // 4, :, (k % 4) * ATT : (k % 4 + 1) * ATT], NT, preferred_element_type=f32
            )
        return (total + part).astype(bf16)

    def att_ref(layer):
        return lambda k: att.at[layer, k]

    def hid_ref(k):
        return hid.at[k]

    def out_ref(k):
        return out.at[k]

    start_exchange()
    start_second()
    load_x.wait()
    normalize(0, lambda rows, j: xin[rows, j * CHUNK : (j + 1) * CHUNK])
    pack_q(0)
    q1(0)
    pack_o(0)
    q2(0)
    pack_o(1)
    pack_q(1)
    q3(0)
    o1(0)
    q4(0)
    q5(0)
    project_in(0)
    o2(0)
    q1(1)
    attend(0)
    load_kv(1)
    o3(0)
    g1(0, att_ref(0))
    q2(1)
    g2(0, att_ref(0))
    o4(0)
    q3(1)
    g3(0, att_ref(0))
    o1(1)
    o5(0)
    g4(0, att_ref(0))
    hid[t] = project_out(0, resid[...])
    g1(1, hid_ref)
    q4(1)
    o2(1)
    g2(1, hid_ref)
    q5(1)
    o3(1)
    g3(1, hid_ref)
    o4(1)
    g4(1, hid_ref)
    normalize(1, lambda rows, j: hid[j, rows, :])
    project_in(1)
    attend(1)
    g1(2, att_ref(1))
    g2(2, att_ref(1))
    g3(2, att_ref(1))
    o5(1)
    g4(2, att_ref(1))
    hown[...] = project_out(1, hid[t])
    keep = pltpu.make_async_copy(hown, out.at[t], loc.at[3])
    keep.start()
    g1(3, out_ref, hown)
    g2(3, out_ref)
    g3(3, out_ref)
    g4(3, out_ref)
    keep.wait()
    for copy in sent:
        copy.wait_send()

    @pl.when(half_of_t != c)
    def _():
        sibling_slab().wait_send()


def fused(*operands):
    whole = pl.BlockSpec(memory_space=pltpu.VMEM)
    anywhere = pl.BlockSpec(memory_space=pl.ANY)
    dma = pltpu.SemaphoreType.DMA
    return pl.pallas_call(
        kernel,
        out_shape=jax.ShapeDtypeStruct((TP, FLAT, CHUNK), bf16),
        in_specs=[anywhere] * 3 + [whole] * 7 + [anywhere] * 2,
        out_specs=anywhere,
        scratch_shapes=[
            pltpu.VMEM((LAYERS, CHUNKS, CHUNK, GROUP), bf16),
            pltpu.VMEM((LAYERS, 2, CHUNK, HALF), bf16),
            pltpu.VMEM((LAYERS, TP, PAD, GROUP), bf16),
            pltpu.VMEM((LAYERS, 2, PAD, HALF), bf16),
            pltpu.VMEM((TP * OWN, GROUP), f32),
            pltpu.VMEM((FLAT, D), bf16),
            pltpu.VMEM((CHUNKS, FLAT, CHUNK), bf16),
            pltpu.VMEM((TP, FLAT, CHUNK), bf16),
            pltpu.VMEM((FLAT, CHUNK), bf16),
            pltpu.VMEM((LAYERS, TP, FLAT, ATT), bf16),
            pltpu.VMEM((ROWS, SLOTS, HEAD), bf16),
            pltpu.VMEM((ROWS, SLOTS, HEAD), bf16),
            pltpu.VMEM((16 * ROWS, HEAD), f32),
            pltpu.VMEM((16 * ROWS, HEAD), f32),
            pltpu.VMEM((FLAT, HEAD), f32),
            pltpu.VMEM((FLAT, HEAD), f32),
            pltpu.VMEM((FLAT, GROUP), f32),
            dma((LAYERS, TP)), dma((LAYERS, TP)),
            dma((LAYERS,)), dma((LAYERS, 3)),
            dma((LAYERS, 15)), dma((LAYERS, 15)),
            dma((LAYERS, 16)), dma((LAYERS, 16)),
            dma((4, 7)), dma((4, 7)),
            dma((4,)),
        ],
        compiler_params=pltpu.CompilerParams(
            collective_id=0, has_side_effects=True, vmem_limit_bytes=60 * 1024 * 1024
        ),
    )(*operands)


def on_device(
    inputs, qkv_weight, out_weight, norm_gain, query_gain, key_gain, stored_rotated_keys, stored_cache_values, lengths
):
    t = lax.axis_index("tp")
    flat = inputs.reshape(FLAT, D)
    resid = lax.dynamic_slice_in_dim(flat.reshape(FLAT, 16, TP * OWN), t * OWN, OWN, axis=2).reshape(FLAT, CHUNK)
    qw = jnp.pad(qkv_weight, ((0, 0), (0, PAD - OWN), (0, 0)))
    ow = jnp.pad(out_weight, ((0, 0), (0, PAD - OWN), (0, 0)))
    second = norm_gain[1].reshape(16, TP, OWN).transpose(1, 0, 2).reshape(D)
    gain = jnp.stack([norm_gain[0], second]).reshape(LAYERS, CHUNKS, 1, CHUNK)
    positions = lengths[None, :] + jnp.arange(STEPS, dtype=jnp.int32)[:, None]
    half = HEAD // 2
    frequency = rope_base ** (-jnp.arange(half, dtype=f32) / half)
    angles = (positions.astype(f32)[..., None] * frequency).reshape(FLAT, half)
    cosine, sine = jnp.cos(angles), jnp.sin(angles)
    cosf = jnp.concatenate([cosine, cosine], axis=-1)
    sinf = jnp.concatenate([-sine, sine], axis=-1)
    len16 = jnp.repeat(lengths, 16).reshape(ROWS * 16, 1)
    hidden = fused(
        flat, qw, ow, resid, gain, query_gain.reshape(LAYERS, 1, HEAD), key_gain.reshape(LAYERS, 1, HEAD),
        cosf, sinf, len16,
        stored_rotated_keys.reshape(LAYERS, ROWS, SLOTS, HEAD), stored_cache_values.reshape(LAYERS, ROWS, SLOTS, HEAD),
    )
    natural = hidden.reshape(TP, FLAT, 16, OWN).transpose(1, 2, 0, 3)
    return natural.reshape(STEPS, ROWS, D)


def solution(mesh):
    return jax.shard_map(
        on_device,
        mesh=mesh,
        in_specs=(
            P(None, "rep", None),
            P(None, ("rep", "tp"), None),
            P(None, ("rep", "tp"), None),
            P(),
            P(),
            P(),
            P(None, "rep", "tp", None, None),
            P(None, "rep", "tp", None, None),
            P("rep"),
        ),
        out_specs=P(None, "rep", None),
        check_vma=False,
    )
```

time: 730 us -> 256 us (0.35)
  waiting for transfers between devices: 545 us -> 0 us
  Pallas kernels: 0 us -> 206 us
  local copies, waits for them, and re-layouts: 87.8 us -> 45.2 us
  blocking collectives: 33.3 us -> 0 us
  matrix products: 29.1 us -> 0 us
  other arithmetic: 16.7 us -> 2.05 us
  between operations: 13.6 us -> 0.07 us
    psum x2 -> x0, waiting for transfers between devices: 430 us -> none  [on_device(): summed = lax.psum(projected, 'tp')]
    pallas_call x0 -> x1, Pallas kernels: none -> 206 us  [fused(): pl.pallas_call(kernel, out_shape=jax.ShapeDtypeStruct((TP, FLAT, CHUNK),...]
    all_gather x2 -> x0, waiting for transfers between devices: 114 us -> none  [the longest x1 68.7 us: on_device(): lax.all_gather(block_qkv, 'rep', axis=1, tiled=True)]
    unnamed x40 -> x2, local copies, waits for them, and re-layouts: 44.5 us -> 0.01 us
    all_to_all x2 -> x0, blocking collectives: 33.3 us -> none  [the longest x1 19.8 us: on_device(): lax.all_to_all(qkv_weight, 'tp', split_axis=2, concat_axis=1, tiled=True)]
    dot_general x3 -> x0, local copies, waits for them, and re-layouts: 32.2 us -> none  [on_device(): jnp.dot(normed, rows_qkv[layer_index], preferred_element_type=jnp.float32)]
    dot_general x12 -> x0, matrix products: 29.1 us -> none  [the longest x2 10.3 us: on_device(): lax.dot_general(attended, rows_out[layer_index], (((1,), (1,)), ((), ()))...]
    reshape x0 -> x3, local copies, waits for them, and re-layouts: none -> 27.4 us  [the longest x2 26.5 us: on_device(): return natural.reshape(STEPS, ROWS, D)]
  transfers between devices with their start and end apart: 4 -> 0, of which waited for: 4 -> 0; matrix products, arithmetic and copies ran while one was open for 11% -> 0% of each run, Pallas kernels for 0% -> 0%
where the time goes in v1:
time: 256 us; the launch traced here: 254 us
  Pallas kernels  206 us (80%)
  local copies, waits for them, and re-layouts  45.2 us (18%)
    pallas_call x1, Pallas kernels, fused(): pl.pallas_call(kernel, out_shape=jax.ShapeDtypeStruct((TP, FLAT, CHUNK),...  206 us
    reshape x2, local copies, waits for them, and re-layouts, on_device(): return natural.reshape(STEPS, ROWS, D)  26.5 us

profile of v1, /device:TPU:32, one launch (start us, length us, event | category | flops | bytes accessed | tf_op | source)
XLA Modules:
  0.0 253.8 jit_solution(14548106745808202856)
XLA Ops:
  0.0 0.0 copy-start
  0.0 0.8 broadcast_reduce_fusion
  0.8 0.1 add.30
  0.9 0.1 add.32
  1.0 0.7 broadcast_in_dim.2
  1.7 0.9 fusion.1
  2.7 0.1 reshape_squeeze.3
  2.8 0.1 stack.8
  2.9 0.7 pad_maximum_fusion.2.gain
  3.6 0.5 fusion
  4.1 0.8 pad_maximum_fusion
  5.0 1.1 reshape_reshape.8.len16
  6.0 2.0 pad.9.ow
  8.1 2.3 pad.8.qw
  10.4 0.0 copy-done
  10.4 3.7 %reshape_reshape.6 = bf16[256,16,320]{2,1,0:T(8,128)(2,1)} reshape(bf16[4,64,5120]{2,1,0:T(8,128)(2,1)S(1)} %copy-done) | data formatting | bytes 5242880 | tf_op jit(solution)/shard_map/reshape;reshape | solution.py:498
  14.1 2.0 constant_dynamic-slice_fusion
  16.1 0.8 copy.12
  16.9 0.9 copy.14.resid
  17.8 206.5 %shard_map.91 = bf16[8,256,640]{2,1,0:T(8,128)(2,1)} custom-call(bf16[256,5120]{1,0:T(8,128)(2,1)} %bitcast.15, bf16[2,48,6144]{2,1,0:T(8,128)(2,1)} %pad.8.qw, bf16[2,48,4096]{2,1,0:T(8,128)(2,1)} %pad.9.ow, bf16[256,640]{1,0:T(8,128)(2,1)} %copy.14.resid, f32[2,8,1,640]{3,2,1,0:T(1,128)} %pad_maximum_fusion.2.gain, f32[2,1,128]{2,1,0:T(1,128)} %bitcast.22, ...), custom_call_target="tpu_custom_call" | custom-call | tf_op jit(solution)/shard_map/pallas_call | solution.py:457
  224.3 3.0 %copy.16 = bf16[8,256,640]{1,2,0:T(8,128)(2,1)S(1)} copy(bf16[8,256,640]{2,1,0:T(8,128)(2,1)} %shard_map.91) | data formatting | bytes 5242880 | tf_op jit(solution)/shard_map/pallas_call | solution.py:457
  227.3 12.2 %copy.19 = bf16[256,16,8,40]{3,2,1,0:T(8,128)(2,1)} copy(bf16[256,16,8,40]{0,3,1,2:T(8,128)(2,1)S(1)} %bitcast.16) | data formatting | bytes 5242880 | tf_op jit(solution)/shard_map/reshape | solution.py:517
  239.4 14.3 %reshape.63 = bf16[4,64,5120]{2,1,0:T(8,128)(2,1)} reshape(bf16[256,16,8,40]{3,2,1,0:T(8,128)(2,1)} %copy.19) | data formatting | bytes 5242880 | tf_op jit(solution)/shard_map/reshape | solution.py:517
  (4 shorter events, 0.0 us)
Async XLA Ops:
  0.0 10.4 %copy-start = (bf16[4,64,5120]{2,1,0:T(8,128)(2,1)S(1)}, bf16[4,64,5120]{2,1,0:T(8,128)(2,1)}, u32[]{:S(2)}) copy-start(bf16[4,64,5120]{2,1,0:T(8,128)(2,1)} %param.9) | copy-start | bytes 7864324

commit v2 on v1

--- a/solution.py
+++ b/solution.py
@@ -15,6 +15,9 @@
 STEPS = 4
 ROWS = 64
 FLAT = STEPS * ROWS
+PARTS = 2
+SIDE = ROWS // PARTS
+PART = FLAT // PARTS
 D = 5120
 CHUNKS = 8
 CHUNK = D // CHUNKS
@@ -33,9 +36,9 @@
 
 
 def kernel(
-    x_hbm, qw, ow, resid, gain, qgain, kgain, cosf, sinf, len16, k_hbm, v_hbm,
+    x_hbm, qw, ow, gains, qgain, kgain, rows_len, frequency, k_hbm, v_hbm,
     out,
-    wq, wo, land_q, land_o, pack, xin, norm, hid, hown, att, kbuf, vbuf, qs, ao, nk, nv, mixed,
+    wq, wo, land_q, land_o, pack, xin, norm, hid, hown, att, kbuf, vbuf, qs, ao, nk, nv, mixed, resid, gain, cosf, sinf, limit,
     a2a_s, a2a_r, ex_s, ex_r, q_s, q_r, o_s, o_r, g_s, g_r, loc,
 ):
     r = lax.axis_index("rep")
@@ -84,8 +87,15 @@
         pl.semaphore_signal(barrier, inc=1, device_id=dev, device_id_type=MESH)
     pl.semaphore_wait(barrier, len(greet))
 
-    load_x = pltpu.make_async_copy(x_hbm, xin, loc.at[0])
-    load_x.start()
+    load_x = [
+        pltpu.make_async_copy(
+            x_hbm.at[s, pl.ds(h * SIDE, SIDE)], xin.at[pl.ds(h * PART + s * SIDE, SIDE)], loc.at[4 + h * STEPS + s]
+        )
+        for h in range(PARTS)
+        for s in range(STEPS)
+    ]
+    for copy in load_x:
+        copy.start()
     kv = {}
 
     def load_kv(layer):
@@ -99,12 +109,14 @@
     def qcols(other):
         return pl.ds(pl.multiple_of(other * GROUP, GROUP), GROUP)
 
+    slab = first, second = pl.ds(0, PAD), pl.ds(2 * OWN - PAD, PAD)
+    skip = (0, PAD - OWN)
     half_of_t = lax.div(t, 4)
     slot1 = lax.rem(t, 4) * 2 + c
     for k in range(1, TP):
         other = lax.rem(t + k, TP)
-        send(qw.at[0, :, qcols(other)], land_q.at[0, t], a2a_s.at[0, k], a2a_r.at[0, t], (r, other))
-    own0 = pltpu.make_async_copy(qw.at[0, :, qcols(t)], land_q.at[0, t], a2a_r.at[0, t])
+        send(qw.at[first, qcols(other)], land_q.at[0, t], a2a_s.at[0, k], a2a_r.at[0, t], (r, other))
+    own0 = pltpu.make_async_copy(qw.at[first, qcols(t)], land_q.at[0, t], a2a_r.at[0, t])
     own0.start()
     load_kv(0)
 
@@ -112,12 +124,12 @@
         for layer in range(LAYERS):
             theirs = pl.ds(pl.multiple_of((1 - c) * HALF, HALF), HALF)
             mine = pl.ds(pl.multiple_of(c * HALF, HALF), HALF)
-            send(ow.at[layer, :, theirs], land_o.at[layer, c], ex_s.at[layer], ex_r.at[layer, c], dev_sib)
-            pltpu.make_async_copy(ow.at[layer, :, mine], land_o.at[layer, c], ex_r.at[layer, 2]).start()
+            send(ow.at[slab[layer], theirs], land_o.at[layer, c], ex_s.at[layer], ex_r.at[layer, c], dev_sib)
+            pltpu.make_async_copy(ow.at[slab[layer], mine], land_o.at[layer, c], ex_r.at[layer, 2]).start()
 
     def sibling_slab():
         return pltpu.make_async_remote_copy(
-            src_ref=qw.at[1, :, qcols(t)], dst_ref=land_q.at[1, slot1], send_sem=a2a_s.at[1, 0],
+            src_ref=qw.at[second, qcols(t)], dst_ref=land_q.at[1, slot1], send_sem=a2a_s.at[1, 0],
             recv_sem=a2a_r.at[1, slot1], device_id=dev_sib, device_id_type=MESH,
         )
 
@@ -125,13 +137,13 @@
         for k in range(1, TP):
             other = lax.rem(t + k, TP)
             send(
-                qw.at[1, :, qcols(other)], land_q.at[1, slot1], a2a_s.at[1, k], a2a_r.at[1, slot1],
+                qw.at[second, qcols(other)], land_q.at[1, slot1], a2a_s.at[1, k], a2a_r.at[1, slot1],
                 (rep(y, zh, half_of_t), other),
             )
 
         @pl.when(half_of_t == c)
         def _():
-            pltpu.make_async_copy(qw.at[1, :, qcols(t)], land_q.at[1, slot1], a2a_r.at[1, slot1]).start()
+            pltpu.make_async_copy(qw.at[second, qcols(t)], land_q.at[1, slot1], a2a_r.at[1, slot1]).start()
 
         @pl.when(half_of_t != c)
         def _():
@@ -141,7 +153,7 @@
         for slot in range(TP):
             got(land_q.at[layer, slot], a2a_r.at[layer, slot])
         for slot in range(TP):
-            pack[slot * OWN : (slot + 1) * OWN, :] = land_q[layer, slot].astype(f32)[:OWN]
+            pack[slot * OWN : (slot + 1) * OWN, :] = land_q[layer, slot].astype(f32)[skip[layer] : skip[layer] + OWN]
         if layer == 0:
             wq[0, p, pl.ds(pl.multiple_of(c * 320, 320), 320), :] = pack[...].astype(bf16)
         else:
@@ -149,12 +161,12 @@
                 wq[1, 4 * c + k, pl.ds(pl.multiple_of(p * 80, 80), 80), :] = pack[k * 80 : (k + 1) * 80, :].astype(bf16)
 
     def pack_o(layer):
-        pltpu.make_async_copy(ow.at[layer, :, pl.ds(0, HALF)], land_o.at[layer, c], ex_r.at[layer, 2]).wait()
+        pltpu.make_async_copy(ow.at[slab[layer], pl.ds(0, HALF)], land_o.at[layer, c], ex_r.at[layer, 2]).wait()
         got(land_o.at[layer, 1 - c], ex_r.at[layer, 1 - c])
         for cut in range(4):
             cols = slice(cut * 512, (cut + 1) * 512)
             both = jnp.concatenate(
-                [land_o[layer, core, :, cols].astype(f32)[:OWN] for core in range(2)], axis=0
+                [land_o[layer, core, :, cols].astype(f32)[skip[layer] : skip[layer] + OWN] for core in range(2)], axis=0
             )
             wo[layer, c, pl.ds(pl.multiple_of(p * 80, 80), 80), cols] = both.astype(bf16)
 
@@ -290,39 +302,78 @@
         g_got(n, ref, 2, 0, 5)
         g_got(n, ref, 2, 1, 6)
 
-    def normalize(layer, read):
+    def prepare():
+        diagonal = lax.broadcasted_iota(jnp.int32, (ROWS, ROWS), 0) == lax.broadcasted_iota(jnp.int32, (ROWS, ROWS), 1)
+        length = jnp.sum(
+            jnp.where(diagonal, jnp.broadcast_to(rows_len[...].astype(f32), (ROWS, ROWS)), 0.0), axis=1, keepdims=True
+        )
+        limit[...] = jnp.broadcast_to(length, (ROWS, SLOTS))
+        flip = jnp.where(lax.broadcasted_iota(jnp.int32, (1, HEAD), 1) < HEAD // 2, -1.0, 1.0)
+        for h in range(PARTS):
+            for s in range(STEPS):
+                angles = (length[h * SIDE : (h + 1) * SIDE] + float(s)) * frequency[...]
+                rows = slice(h * PART + s * SIDE, h * PART + (s + 1) * SIDE)
+                cosf[rows, :] = jnp.cos(angles)
+                sinf[rows, :] = jnp.sin(angles) * flip
+        for j in range(CHUNKS):
+            gain[j : j + 1, :] = gains[0:1, j * CHUNK : (j + 1) * CHUNK]
+            gain[CHUNKS + j : CHUNKS + j + 1, :] = jnp.concatenate(
+                [gains[1:2, k * 320 + j * OWN : k * 320 + (j + 1) * OWN] for k in range(16)], axis=1
+            )
+
+    def pick_own():
+        src = lax.broadcasted_iota(jnp.int32, (CHUNK, 256), 0)
+        dst = lax.broadcasted_iota(jnp.int32, (CHUNK, 256), 1)
+        for j in range(CHUNKS):
+            base, shift = j * 80 // 128 * 128, j * 80 % 128
+            place = dst - shift
+            wanted = jnp.where(place < OWN, place + t * OWN, place + (320 - OWN) + t * OWN)
+            ok = jnp.logical_and(jnp.logical_and(place >= 0, place < 2 * OWN), src == wanted)
+            pick = jnp.where(ok, 1.0, 0.0).astype(bf16)
+            mine = jnp.dot(xin[:, j * CHUNK : (j + 1) * CHUNK], pick, preferred_element_type=f32)
+            width = min(256, CHUNK - base)
+            if j == 0:
+                resid[...] = jnp.zeros_like(resid)
+            resid[:, base : base + width] += mine[:, :width]
+
+    def normalize(layer, start, count, read):
         def body(b, carry):
             rows = pl.ds(pl.multiple_of(b * 32, 32), 32)
+            inside = pl.ds(pl.multiple_of(b * 32 - start, 32), 32)
             total = jnp.zeros((32, 1), f32)
             for j in range(CHUNKS):
-                wide = read(rows, j).astype(f32)
+                wide = read(inside, j).astype(f32)
                 total = total + jnp.sum(wide * wide, axis=-1, keepdims=True)
             scale = lax.rsqrt(total * (1.0 / D) + epsilon)
             for j in range(CHUNKS):
-                norm[j, rows, :] = (read(rows, j).astype(f32) * scale * gain[layer, j]).astype(bf16)
+                norm[j, rows, :] = (read(inside, j).astype(f32) * scale * gain[layer * CHUNKS + j : layer * CHUNKS + j + 1, :]).astype(bf16)
             return carry
 
-        lax.fori_loop(0, FLAT // 32, body, 0)
-
-    def project_in(layer):
-        mixed[...] = jnp.zeros_like(mixed)
+        lax.fori_loop(start // 32, (start + count) // 32, body, 0)
+
+    def project_in(layer, start, count):
+        rows = slice(start, start + count)
+        mixed[rows, :] = jnp.zeros((count, GROUP), f32)
 
         def body(j, carry):
-            mixed[...] += jnp.dot(norm[j], wq[layer, j], preferred_element_type=f32)
+            mixed[rows, :] += jnp.dot(norm[j, rows], wq[layer, j], preferred_element_type=f32)
             return carry
 
         lax.fori_loop(0, CHUNKS, body, 0)
 
         def turn(v, g):
             n = v * lax.rsqrt(jnp.mean(v * v, axis=-1, keepdims=True) + epsilon) * g
-            return n * cosf[...] + pltpu.roll(n, HEAD // 2, 1) * sinf[...]
+            return n * cosf[rows, :] + pltpu.roll(n, HEAD // 2, 1) * sinf[rows, :]
 
         for i in range(4):
-            q = turn(mixed[:, i * HEAD : (i + 1) * HEAD], qgain[layer])
-            for s in range(STEPS):
-                qs[(s * 4 + i) * ROWS : (s * 4 + i + 1) * ROWS, :] = q[s * ROWS : (s + 1) * ROWS]
-        nk[...] = turn(mixed[:, 4 * HEAD : 5 * HEAD], kgain[layer])
-        nv[...] = mixed[:, 5 * HEAD : 6 * HEAD]
+            q = turn(mixed[rows, i * HEAD : (i + 1) * HEAD], qgain[layer])
+            for h in range(start // PART, (start + count) // PART):
+                for s in range(STEPS):
+                    at = h * PART + s * SIDE - start
+                    to = (s * 4 + i) * ROWS + h * SIDE
+                    qs[to : to + SIDE, :] = q[at : at + SIDE]
+        nk[rows, :] = turn(mixed[rows, 4 * HEAD : 5 * HEAD], kgain[layer])
+        nv[rows, :] = mixed[rows, 5 * HEAD : 6 * HEAD]
 
     row = lax.broadcasted_iota(jnp.int32, (128, 32), 0)
     col = lax.broadcasted_iota(jnp.int32, (128, 32), 1)
@@ -330,23 +381,24 @@
         jnp.right_shift(row, 4) == jnp.bitwise_and(col, 7),
         jnp.right_shift(col, 3) <= jnp.bitwise_and(jnp.right_shift(row, 2), 3),
     )
-    slot_index = lax.broadcasted_iota(jnp.int32, (128, SLOTS), 1)
-
-    def attend(layer):
-        for copy in kv[layer]:
-            copy.wait()
+    slot_index = lax.broadcasted_iota(jnp.int32, (16, SLOTS), 1).astype(f32)
+
+    def attend(layer, h):
+        if h == 0:
+            for copy in kv[layer]:
+                copy.wait()
 
         def body(g, carry):
             q = [qs[pl.ds(g * 8 + k, 16, stride=ROWS), :].astype(bf16) for k in range(8)]
-            old = jnp.concatenate(
-                [lax.dot_general(q[k], kbuf[g * 8 + k], NT, preferred_element_type=f32) for k in range(8)], axis=0
-            ) * HEAD ** (-0.5)
-            part = [pl.ds(pl.multiple_of(s * ROWS + g * 8, 8), 8) for s in range(STEPS)]
+            old = []
+            for k in range(8):
+                score = lax.dot_general(q[k], kbuf[g * 8 + k], NT, preferred_element_type=f32) * HEAD ** (-0.5)
+                old.append(jnp.where(slot_index < limit[pl.ds(g * 8 + k, 1), :], score, -jnp.inf))
+            old = jnp.concatenate(old, axis=0)
+            part = [pl.ds(pl.multiple_of(h * (PART - SIDE) + s * SIDE + g * 8, 8), 8) for s in range(STEPS)]
             keys = jnp.concatenate([nk[w, :] for w in part], axis=0).astype(bf16)
             values = jnp.concatenate([nv[w, :] for w in part], axis=0).astype(bf16)
             new = lax.dot_general(jnp.concatenate(q, axis=0), keys, NT, preferred_element_type=f32) * HEAD ** (-0.5)
-            live = slot_index < len16[pl.ds(pl.multiple_of(g * 128, 128), 128), :]
-            old = jnp.where(live, old, -jnp.inf)
             new = jnp.where(fresh, new, -jnp.inf)
             top = jnp.maximum(jnp.max(old, axis=-1, keepdims=True), jnp.max(new, axis=-1, keepdims=True))
             old = jnp.exp(old - top)
@@ -362,86 +414,128 @@
                 )
             return carry
 
-        lax.fori_loop(0, ROWS // 8, body, 0)
+        lax.fori_loop(h * SIDE // 8, (h + 1) * SIDE // 8, body, 0)
         for s in range(STEPS):
             for i in range(4):
-                att[layer, t, s * ROWS : (s + 1) * ROWS, i * HEAD : (i + 1) * HEAD] = ao[
-                    (s * 4 + i) * ROWS : (s * 4 + i + 1) * ROWS, :
+                start = (s * 4 + i) * ROWS + h * SIDE
+                att[layer, h, t, s * SIDE : (s + 1) * SIDE, i * HEAD : (i + 1) * HEAD] = ao[
+                    start : start + SIDE, :
                 ].astype(bf16)
 
-    def project_out(layer, before):
-        total = before.astype(f32)
-        part = jnp.zeros((FLAT, CHUNK), f32)
+    def project_out(layer, h, before):
+        total = jnp.zeros((PART, CHUNK), f32)
         for k in range(TP):
-            part = part + lax.dot_general(
-                att[layer, k], wo[layer, k // 4, :, (k % 4) * ATT : (k % 4 + 1) * ATT], NT, preferred_element_type=f32
+            total = total + lax.dot_general(
+                att[layer, h, k], wo[layer, k // 4, :, (k % 4) * ATT : (k % 4 + 1) * ATT], NT,
+                preferred_element_type=f32,
             )
-        return (total + part).astype(bf16)
-
-    def att_ref(layer):
-        return lambda k: att.at[layer, k]
-
-    def hid_ref(k):
-        return hid.at[k]
-
-    def out_ref(k):
-        return out.at[k]
+        return (before.astype(f32) + total).astype(bf16)
+
+    def att_ref(layer, h):
+        return lambda k: att.at[layer, h, k]
+
+    def hid_ref(h):
+        return lambda k: hid.at[h, k]
+
+    def out_ref(h):
+        return lambda k: out.at[h, k]
+
+    refs = [
+        att_ref(0, 0), att_ref(0, 1), hid_ref(0), hid_ref(1), att_ref(1, 0), att_ref(1, 1), out_ref(0), out_ref(1)
+    ]
+
+    def g(step, n, own=None):
+        if step == 1:
+            g1(n, refs[n], own)
+        else:
+            (g2, g3, g4)[step - 2](n, refs[n])
+
+    def first_out(h):
+        hid[h, t] = project_out(0, h, resid[h * PART : (h + 1) * PART, :])
+        g(1, 2 + h)
+
+    def second_in(h):
+        normalize(1, h * PART, PART, lambda rows, j: hid[h, j, rows, :])
+        project_in(1, h * PART, PART)
+        attend(1, h)
+        g(1, 4 + h)
+
+    keep = [pltpu.make_async_copy(hown.at[h], out.at[h, t], loc.at[3 * h]) for h in range(PARTS)]
+
+    def second_out(h):
+        hown[h] = project_out(1, h, hid[h, t])
+        g(1, 6 + h, hown.at[h])
+        keep[h].start()
 
     start_exchange()
-    start_second()
-    load_x.wait()
-    normalize(0, lambda rows, j: xin[rows, j * CHUNK : (j + 1) * CHUNK])
+    prepare()
+    pack_o(0)
+    o1(0)
+    for copy in load_x:
+        copy.wait()
+    pick_own()
+    normalize(0, 0, FLAT, lambda rows, j: xin[rows, j * CHUNK : (j + 1) * CHUNK])
     pack_q(0)
     q1(0)
-    pack_o(0)
+    start_second()
+    pack_o(1)
     q2(0)
-    pack_o(1)
+    o2(0)
+    q3(0)
     pack_q(1)
-    q3(0)
-    o1(0)
+    q1(1)
+    o3(0)
     q4(0)
     q5(0)
-    project_in(0)
-    o2(0)
-    q1(1)
-    attend(0)
+    project_in(0, 0, FLAT)
+    attend(0, 0)
+    g(1, 0)
+    attend(0, 1)
+    g(1, 1)
     load_kv(1)
-    o3(0)
-    g1(0, att_ref(0))
+    g(2, 0)
     q2(1)
-    g2(0, att_ref(0))
+    g(2, 1)
+    g(3, 0)
     o4(0)
+    o5(0)
+    g(3, 1)
+    g(4, 0)
+    first_out(0)
     q3(1)
-    g3(0, att_ref(0))
+    g(4, 1)
+    first_out(1)
     o1(1)
-    o5(0)
-    g4(0, att_ref(0))
-    hid[t] = project_out(0, resid[...])
-    g1(1, hid_ref)
+    g(2, 2)
+    g(2, 3)
+    g(3, 2)
     q4(1)
+    q5(1)
+    g(4, 2)
     o2(1)
-    g2(1, hid_ref)
-    q5(1)
+    second_in(0)
+    g(3, 3)
+    g(4, 3)
+    second_in(1)
+    g(2, 4)
+    g(2, 5)
+    g(3, 4)
     o3(1)
-    g3(1, hid_ref)
     o4(1)
-    g4(1, hid_ref)
-    normalize(1, lambda rows, j: hid[j, rows, :])
-    project_in(1)
-    attend(1)
-    g1(2, att_ref(1))
-    g2(2, att_ref(1))
-    g3(2, att_ref(1))
+    g(3, 5)
     o5(1)
-    g4(2, att_ref(1))
-    hown[...] = project_out(1, hid[t])
-    keep = pltpu.make_async_copy(hown, out.at[t], loc.at[3])
-    keep.start()
-    g1(3, out_ref, hown)
-    g2(3, out_ref)
-    g3(3, out_ref)
-    g4(3, out_ref)
-    keep.wait()
+    g(4, 4)
+    second_out(0)
+    g(4, 5)
+    second_out(1)
+    g(2, 6)
+    g(2, 7)
+    g(3, 6)
+    g(3, 7)
+    g(4, 6)
+    g(4, 7)
+    for copy in keep:
+        copy.wait()
     for copy in sent:
         copy.wait_send()
 
@@ -456,8 +550,8 @@
     dma = pltpu.SemaphoreType.DMA
     return pl.pallas_call(
         kernel,
-        out_shape=jax.ShapeDtypeStruct((TP, FLAT, CHUNK), bf16),
-        in_specs=[anywhere] * 3 + [whole] * 7 + [anywhere] * 2,
+        out_shape=jax.ShapeDtypeStruct((PARTS, TP, PART, CHUNK), bf16),
+        in_specs=[anywhere] * 3 + [whole] * 5 + [anywhere] * 2,
         out_specs=anywhere,
         scratch_shapes=[
             pltpu.VMEM((LAYERS, CHUNKS, CHUNK, GROUP), bf16),
@@ -467,9 +561,9 @@
             pltpu.VMEM((TP * OWN, GROUP), f32),
             pltpu.VMEM((FLAT, D), bf16),
             pltpu.VMEM((CHUNKS, FLAT, CHUNK), bf16),
-            pltpu.VMEM((TP, FLAT, CHUNK), bf16),
-            pltpu.VMEM((FLAT, CHUNK), bf16),
-            pltpu.VMEM((LAYERS, TP, FLAT, ATT), bf16),
+            pltpu.VMEM((PARTS, TP, PART, CHUNK), bf16),
+            pltpu.VMEM((PARTS, PART, CHUNK), bf16),
+            pltpu.VMEM((LAYERS, PARTS, TP, PART, ATT), bf16),
             pltpu.VMEM((ROWS, SLOTS, HEAD), bf16),
             pltpu.VMEM((ROWS, SLOTS, HEAD), bf16),
             pltpu.VMEM((16 * ROWS, HEAD), f32),
@@ -477,12 +571,17 @@
             pltpu.VMEM((FLAT, HEAD), f32),
             pltpu.VMEM((FLAT, HEAD), f32),
             pltpu.VMEM((FLAT, GROUP), f32),
+            pltpu.VMEM((FLAT, CHUNK), f32),
+            pltpu.VMEM((LAYERS * CHUNKS, CHUNK), f32),
+            pltpu.VMEM((FLAT, HEAD), f32),
+            pltpu.VMEM((FLAT, HEAD), f32),
+            pltpu.VMEM((ROWS, SLOTS), f32),
             dma((LAYERS, TP)), dma((LAYERS, TP)),
             dma((LAYERS,)), dma((LAYERS, 3)),
             dma((LAYERS, 15)), dma((LAYERS, 15)),
             dma((LAYERS, 16)), dma((LAYERS, 16)),
-            dma((4, 7)), dma((4, 7)),
-            dma((4,)),
+            dma((4 * PARTS, 7)), dma((4 * PARTS, 7)),
+            dma((4 + PARTS * STEPS,)),
         ],
         compiler_params=pltpu.CompilerParams(
             collective_id=0, has_side_effects=True, vmem_limit_bytes=60 * 1024 * 1024
@@ -490,31 +589,44 @@
     )(*operands)
 
 
+def restore_kernel(hidden, natural):
+    for p in range(CHUNKS):
+        window = slice(p * 80 // 128 * 128, -(-(p + 1) * 80 // 128) * 128)
+        wide = [hidden[0, k, :, window].astype(f32) for k in range(TP)]
+        start = p * 80 % 128
+        parts = [wide[k][:, start + core * OWN : start + (core + 1) * OWN] for core in range(2) for k in range(TP)]
+        natural[0, :, p * CHUNK : (p + 1) * CHUNK] = jnp.concatenate(parts, axis=1).astype(bf16)
+
+
+def restore(hidden):
+    return pl.pallas_call(
+        restore_kernel,
+        out_shape=jax.ShapeDtypeStruct((STEPS, ROWS, D), bf16),
+        grid=(PARTS, STEPS),
+        in_specs=[pl.BlockSpec((1, TP, SIDE, CHUNK), lambda h, s: (h, 0, s, 0))],
+        out_specs=pl.BlockSpec((1, SIDE, D), lambda h, s: (s, h, 0)),
+        compiler_params=pltpu.CompilerParams(vmem_limit_bytes=32 * 1024 * 1024),
+    )(hidden)
+
+
 def on_device(
     inputs, qkv_weight, out_weight, norm_gain, query_gain, key_gain, stored_rotated_keys, stored_cache_values, lengths
 ):
-    t = lax.axis_index("tp")
-    flat = inputs.reshape(FLAT, D)
-    resid = lax.dynamic_slice_in_dim(flat.reshape(FLAT, 16, TP * OWN), t * OWN, OWN, axis=2).reshape(FLAT, CHUNK)
-    qw = jnp.pad(qkv_weight, ((0, 0), (0, PAD - OWN), (0, 0)))
-    ow = jnp.pad(out_weight, ((0, 0), (0, PAD - OWN), (0, 0)))
-    second = norm_gain[1].reshape(16, TP, OWN).transpose(1, 0, 2).reshape(D)
-    gain = jnp.stack([norm_gain[0], second]).reshape(LAYERS, CHUNKS, 1, CHUNK)
-    positions = lengths[None, :] + jnp.arange(STEPS, dtype=jnp.int32)[:, None]
     half = HEAD // 2
     frequency = rope_base ** (-jnp.arange(half, dtype=f32) / half)
-    angles = (positions.astype(f32)[..., None] * frequency).reshape(FLAT, half)
-    cosine, sine = jnp.cos(angles), jnp.sin(angles)
-    cosf = jnp.concatenate([cosine, cosine], axis=-1)
-    sinf = jnp.concatenate([-sine, sine], axis=-1)
-    len16 = jnp.repeat(lengths, 16).reshape(ROWS * 16, 1)
     hidden = fused(
-        flat, qw, ow, resid, gain, query_gain.reshape(LAYERS, 1, HEAD), key_gain.reshape(LAYERS, 1, HEAD),
-        cosf, sinf, len16,
-        stored_rotated_keys.reshape(LAYERS, ROWS, SLOTS, HEAD), stored_cache_values.reshape(LAYERS, ROWS, SLOTS, HEAD),
+        inputs,
+        qkv_weight.reshape(LAYERS * OWN, TP * GROUP),
+        out_weight.reshape(LAYERS * OWN, TP * ATT),
+        norm_gain,
+        query_gain.reshape(LAYERS, 1, HEAD),
+        key_gain.reshape(LAYERS, 1, HEAD),
+        lengths.reshape(1, ROWS),
+        jnp.concatenate([frequency, frequency]).reshape(1, HEAD),
+        stored_rotated_keys.reshape(LAYERS, ROWS, SLOTS, HEAD),
+        stored_cache_values.reshape(LAYERS, ROWS, SLOTS, HEAD),
     )
-    natural = hidden.reshape(TP, FLAT, 16, OWN).transpose(1, 2, 0, 3)
-    return natural.reshape(STEPS, ROWS, D)
+    return restore(hidden)
 
 
 def solution(mesh):

time: 256 us -> 188 us (0.73)
  local copies, waits for them, and re-layouts: 45.2 us -> 1.73 us
  Pallas kernels: 206 us -> 183 us
    reshape x3 -> x0, local copies, waits for them, and re-layouts: 27.4 us -> none  [the longest x2 26.5 us: on_device(): return natural.reshape(STEPS, ROWS, D)]
    pallas_call x1 -> x2, Pallas kernels: 206 us -> 183 us  [the longest x1 178 us: fused(): pl.pallas_call(kernel, out_shape=jax.ShapeDtypeStruct((PARTS, TP, PART, C...]
    another operation x5 -> x0, local copies, waits for them, and re-layouts: 5 us -> none  [the longest x1 3.7 us: on_device(): flat.reshape(FLAT, 16, TP * OWN)]
    pad x2 -> x0, local copies, waits for them, and re-layouts: 4.33 us -> none  [the longest x1 2.3 us: on_device(): qw = jnp.pad(qkv_weight, ((0, 0), (0, PAD - OWN), (0, 0)))]
    pallas_call x1 -> x0, local copies, waits for them, and re-layouts: 2.97 us -> none  [fused(): pl.pallas_call(kernel, out_shape=jax.ShapeDtypeStruct((TP, FLAT, CHUNK),...]
    dynamic_slice x2 -> x0, local copies, waits for them, and re-layouts: 2.81 us -> none  [on_device(): lax.dynamic_slice_in_dim(flat.reshape(FLAT, 16, TP * OWN), t * OWN, OWN,...]
where the time goes in v2:
time: 188 us; the launch traced here: 185 us
  Pallas kernels  183 us (97%)
    pallas_call x1, Pallas kernels, fused(): pl.pallas_call(kernel, out_shape=jax.ShapeDtypeStruct((PARTS, TP, PART, C...  178 us
    pallas_call x1, Pallas kernels, restore(): pl.pallas_call(restore_kernel, out_shape=jax.ShapeDtypeStruct((STEPS, ROW...  5.03 us

profile of v2, /device:TPU:32, one launch (start us, length us, event | category | flops | bytes accessed | tf_op | source)
XLA Modules:
  0.0 185.4 jit_solution(1180668408841963821)
XLA Ops:
  0.0 0.6 maximum_bitcast_fusion.frequency
  0.6 178.0 %shard_map.91.hidden = bf16[2,8,128,640]{3,2,1,0:T(8,128)(2,1)} custom-call(bf16[4,64,5120]{2,1,0:T(8,128)(2,1)} %x_hbm.1, bf16[80,6144]{1,0:T(8,128)(2,1)} %bitcast.11, bf16[80,4096]{1,0:T(8,128)(2,1)} %bitcast.12, f32[2,5120]{1,0:T(2,128)} %gains.1, f32[2,1,128]{2,1,0:T(1,128)} %bitcast.13, f32[2,1,128]{2,1,0:T(1,128)} %bitcast.14, s32[1,64]{1,0:T(1,128)} %bitcast.15, ...), custom_call_target="tpu_custom_call" | custom-call | tf_op jit(solution)/shard_map/pallas_call | solution.py:551
  178.6 0.0 copy-start
  178.6 1.7 copy-done
  180.3 5.0 %shard_map.92 = bf16[4,64,5120]{2,1,0:T(8,128)(2,1)} custom-call(bf16[2,8,128,640]{3,2,1,0:T(8,128)(2,1)S(1)} %copy-done), custom_call_target="tpu_custom_call" | custom-call | tf_op jit(solution)/shard_map/pallas_call | solution.py:602
  (1 shorter events, 0.0 us)
Async XLA Ops:
  178.6 1.7 copy-start

commit v3 on v2

--- a/solution.py
+++ b/solution.py
@@ -32,6 +32,8 @@
 f32 = jnp.float32
 bf16 = jnp.bfloat16
 
+O_Z_FIRST = (True, True)
+G_Z_FIRST = (True, False, True, False, True, False, True, False)
 NT = (((1,), (1,)), ((), ()))
 
 
@@ -180,127 +182,148 @@
     def zsel(e):
         return zh if e == 0 else 1 - zh
 
-    def q_send(layer, d, e, dev, idx):
-        b = qblk(layer, ring_y[d], zsel(e), c)
-        send(b, b, q_s.at[layer, idx], q_r.at[layer, idx], dev)
-
-    def q_got(layer, d, e, idx):
-        got(qblk(layer, ring_y[d], zsel(e), c), q_r.at[layer, idx])
-
-    def q_sib(layer, d, e):
-        q_send(layer, d, e, dev_sib, 7 + d * 2 + e)
-
-    def q1(layer):
-        q_send(layer, 0, 0, dev_z, 0)
-        q_send(layer, 0, 0, dev_yp, 1)
-        q_send(layer, 0, 0, dev_ym, 3)
-        q_sib(layer, 0, 0)
-
-    def q2(layer):
-        q_got(layer, 0, 1, 0)
-        q_send(layer, 0, 1, dev_yp, 2)
-        q_send(layer, 0, 1, dev_ym, 4)
-        q_sib(layer, 0, 1)
-
-    def q3(layer):
-        q_got(layer, 3, 0, 1)
-        q_send(layer, 3, 0, dev_yp, 5)
-        q_sib(layer, 3, 0)
-        q_got(layer, 1, 0, 3)
-        q_sib(layer, 1, 0)
-        q_got(layer, 1, 1, 4)
-        q_send(layer, 1, 1, dev_ym, 6)
-        q_sib(layer, 1, 1)
-        q_got(layer, 3, 1, 2)
-        q_sib(layer, 3, 1)
-
-    def q4(layer):
-        q_got(layer, 2, 0, 5)
-        q_sib(layer, 2, 0)
-        q_got(layer, 2, 1, 6)
-        q_sib(layer, 2, 1)
-
-    def q5(layer):
-        for d in range(4):
-            for e in range(2):
-                got(qblk(layer, ring_y[d], zsel(e), 1 - c), q_r.at[layer, 7 + d * 2 + e])
-
     def oblk(layer, y_, zh_, core, part=None):
         cols = slice(None) if part is None else pl.ds(part * 1024, 1024)
         return wo.at[layer, core, pl.ds(pl.multiple_of((y_ * 2 + zh_) * 80, 80), 80), cols]
 
-    def o_send(layer, d, e, dev, idx, part=None):
-        b = oblk(layer, ring_y[d], zsel(e), c, part)
-        send(b, b, o_s.at[layer, idx], o_r.at[layer, idx], dev)
-
-    def o_got(layer, d, e, idx, part=None):
-        got(oblk(layer, ring_y[d], zsel(e), c, part), o_r.at[layer, idx])
-
-    def o_pass(layer, d):
-        o_send(layer, d, 0, dev_z, 4 + d)
-        o_send(layer, d, 0, dev_sib, 8 + d * 2)
-
-    def o1(layer):
-        o_send(layer, 0, 0, dev_yp, 0)
-        o_send(layer, 0, 0, dev_ym, 1)
-        o_pass(layer, 0)
-
-    def o2(layer):
-        o_got(layer, 3, 0, 0)
-        o_send(layer, 3, 0, dev_yp, 2, 0)
-        o_pass(layer, 3)
-        o_got(layer, 1, 0, 1)
-        o_send(layer, 1, 0, dev_ym, 3, 1)
-        o_pass(layer, 1)
-
-    def o3(layer):
-        o_got(layer, 2, 0, 2, 0)
-        o_got(layer, 2, 0, 3, 1)
-        o_pass(layer, 2)
-
-    def o4(layer):
-        for d in (0, 3, 1, 2):
-            o_got(layer, d, 1, 4 + d)
-            o_send(layer, d, 1, dev_sib, 8 + d * 2 + 1)
-
-    def o5(layer):
-        for d in range(4):
-            for e in range(2):
-                got(oblk(layer, ring_y[d], zsel(e), 1 - c), o_r.at[layer, 8 + d * 2 + e])
+    streams = {
+        ("q", 0): (qblk, q_s, q_r, True),
+        ("q", 1): (qblk, q_s, q_r, True),
+        ("o", 0): (oblk, o_s, o_r, O_Z_FIRST[0]),
+        ("o", 1): (oblk, o_s, o_r, O_Z_FIRST[1]),
+    }
+
+    def w_send(name, d, e, dev, idx, *part):
+        blk, ss, rs, _ = streams[name]
+        b = blk(name[1], ring_y[d], zsel(e), c, *part)
+        send(b, b, ss.at[name[1], idx], rs.at[name[1], idx], dev)
+
+    def w_got(name, d, e, idx, *part):
+        blk, _, rs, _ = streams[name]
+        got(blk(name[1], ring_y[d], zsel(e), c, *part), rs.at[name[1], idx])
+
+    def w_sib(name, d, e):
+        w_send(name, d, e, dev_sib, 8 + d * 2 + e)
+
+    def w_pass(name, d):
+        w_send(name, d, 0, dev_z, 4 + d)
+        w_sib(name, d, 0)
+
+    def w_step(step, name):
+        if step == 5:
+            blk, _, rs, _ = streams[name]
+            for d in range(4):
+                for e in range(2):
+                    got(blk(name[1], ring_y[d], zsel(e), 1 - c), rs.at[name[1], 8 + d * 2 + e])
+        elif streams[name][3]:
+            if step == 1:
+                w_send(name, 0, 0, dev_z, 0)
+                w_send(name, 0, 0, dev_yp, 1)
+                w_send(name, 0, 0, dev_ym, 3)
+                w_sib(name, 0, 0)
+            elif step == 2:
+                w_got(name, 0, 1, 0)
+                w_send(name, 0, 1, dev_yp, 2)
+                w_send(name, 0, 1, dev_ym, 4)
+                w_sib(name, 0, 1)
+            elif step == 3:
+                w_got(name, 3, 0, 1)
+                w_send(name, 3, 0, dev_yp, 5)
+                w_sib(name, 3, 0)
+                w_got(name, 1, 0, 3)
+                w_sib(name, 1, 0)
+                w_got(name, 1, 1, 4)
+                w_send(name, 1, 1, dev_ym, 6)
+                w_sib(name, 1, 1)
+                w_got(name, 3, 1, 2)
+                w_sib(name, 3, 1)
+            else:
+                w_got(name, 2, 0, 5)
+                w_sib(name, 2, 0)
+                w_got(name, 2, 1, 6)
+                w_sib(name, 2, 1)
+        else:
+            if step == 1:
+                w_send(name, 0, 0, dev_yp, 0)
+                w_send(name, 0, 0, dev_ym, 1)
+                w_pass(name, 0)
+            elif step == 2:
+                w_got(name, 3, 0, 0)
+                w_send(name, 3, 0, dev_yp, 2, 0)
+                w_pass(name, 3)
+                w_got(name, 1, 0, 1)
+                w_send(name, 1, 0, dev_ym, 3, 1)
+                w_pass(name, 1)
+            elif step == 3:
+                w_got(name, 2, 0, 2, 0)
+                w_got(name, 2, 0, 3, 1)
+                w_pass(name, 2)
+            else:
+                for d in (0, 3, 1, 2):
+                    w_got(name, d, 1, 4 + d)
+                    w_sib(name, d, 1)
+
+    def q(step, layer):
+        w_step(step, ("q", layer))
+
+    def o(step, layer):
+        w_step(step, ("o", layer))
 
     ring_x = [x, xp, lax.rem(x + 2, 4), xm]
 
     def tsel(d, e):
         return ring_x[d] * 2 + (zl if e == 0 else 1 - zl)
 
-    def g_send(n, ref, d, e, dev, idx, own=None):
-        b = ref(tsel(d, e))
+    def g_blk(n, d, e, part):
+        b = refs[n](tsel(d, e))
+        return b if part is None else b.at[pl.ds(part * (PART // 2), PART // 2)]
+
+    def g_send(n, d, e, dev, idx, own=None, part=None):
+        b = g_blk(n, d, e, part)
         send(b if own is None else own, b, g_s.at[n, idx], g_r.at[n, idx], dev)
 
-    def g_got(n, ref, d, e, idx):
-        got(ref(tsel(d, e)), g_r.at[n, idx])
-
-    def g1(n, ref, own=None):
-        g_send(n, ref, 0, 0, dev_zl, 0, own)
-        g_send(n, ref, 0, 0, dev_xp, 1, own)
-        g_send(n, ref, 0, 0, dev_xm, 3, own)
-
-    def g2(n, ref):
-        g_got(n, ref, 0, 1, 0)
-        g_send(n, ref, 0, 1, dev_xp, 2)
-        g_send(n, ref, 0, 1, dev_xm, 4)
-
-    def g3(n, ref):
-        g_got(n, ref, 3, 0, 1)
-        g_send(n, ref, 3, 0, dev_xp, 5)
-        g_got(n, ref, 1, 0, 3)
-        g_got(n, ref, 1, 1, 4)
-        g_send(n, ref, 1, 1, dev_xm, 6)
-        g_got(n, ref, 3, 1, 2)
-
-    def g4(n, ref):
-        g_got(n, ref, 2, 0, 5)
-        g_got(n, ref, 2, 1, 6)
+    def g_got(n, d, e, idx, part=None):
+        got(g_blk(n, d, e, part), g_r.at[n, idx])
+
+    def g(step, n, own=None):
+        if G_Z_FIRST[n]:
+            if step == 1:
+                g_send(n, 0, 0, dev_zl, 0, own)
+                g_send(n, 0, 0, dev_xp, 1, own)
+                g_send(n, 0, 0, dev_xm, 3, own)
+            elif step == 2:
+                g_got(n, 0, 1, 0)
+                g_send(n, 0, 1, dev_xp, 2)
+                g_send(n, 0, 1, dev_xm, 4)
+            elif step == 3:
+                g_got(n, 3, 0, 1)
+                g_send(n, 3, 0, dev_xp, 5)
+                g_got(n, 1, 0, 3)
+                g_got(n, 1, 1, 4)
+                g_send(n, 1, 1, dev_xm, 6)
+                g_got(n, 3, 1, 2)
+            else:
+                g_got(n, 2, 0, 5)
+                g_got(n, 2, 1, 6)
+        else:
+            if step == 1:
+                g_send(n, 0, 0, dev_xp, 0, own)
+                g_send(n, 0, 0, dev_xm, 1, own)
+                g_send(n, 0, 0, dev_zl, 4, own)
+            elif step == 2:
+                g_got(n, 3, 0, 0)
+                g_send(n, 3, 0, dev_xp, 2, part=0)
+                g_send(n, 3, 0, dev_zl, 7)
+                g_got(n, 1, 0, 1)
+                g_send(n, 1, 0, dev_xm, 3, part=1)
+                g_send(n, 1, 0, dev_zl, 5)
+            elif step == 3:
+                g_got(n, 2, 0, 2, 0)
+                g_got(n, 2, 0, 3, 1)
+                g_send(n, 2, 0, dev_zl, 6)
+            else:
+                for d in range(4):
+                    g_got(n, d, 1, 4 + d)
 
     def prepare():
         diagonal = lax.broadcasted_iota(jnp.int32, (ROWS, ROWS), 0) == lax.broadcasted_iota(jnp.int32, (ROWS, ROWS), 1)
@@ -366,12 +389,12 @@
             return n * cosf[rows, :] + pltpu.roll(n, HEAD // 2, 1) * sinf[rows, :]
 
         for i in range(4):
-            q = turn(mixed[rows, i * HEAD : (i + 1) * HEAD], qgain[layer])
+            turned = turn(mixed[rows, i * HEAD : (i + 1) * HEAD], qgain[layer])
             for h in range(start // PART, (start + count) // PART):
                 for s in range(STEPS):
                     at = h * PART + s * SIDE - start
                     to = (s * 4 + i) * ROWS + h * SIDE
-                    qs[to : to + SIDE, :] = q[at : at + SIDE]
+                    qs[to : to + SIDE, :] = turned[at : at + SIDE]
         nk[rows, :] = turn(mixed[rows, 4 * HEAD : 5 * HEAD], kgain[layer])
         nv[rows, :] = mixed[rows, 5 * HEAD : 6 * HEAD]
 
@@ -388,17 +411,17 @@
             for copy in kv[layer]:
                 copy.wait()
 
-        def body(g, carry):
-            q = [qs[pl.ds(g * 8 + k, 16, stride=ROWS), :].astype(bf16) for k in range(8)]
+        def body(b, carry):
+            query = [qs[pl.ds(b * 8 + k, 16, stride=ROWS), :].astype(bf16) for k in range(8)]
             old = []
             for k in range(8):
-                score = lax.dot_general(q[k], kbuf[g * 8 + k], NT, preferred_element_type=f32) * HEAD ** (-0.5)
-                old.append(jnp.where(slot_index < limit[pl.ds(g * 8 + k, 1), :], score, -jnp.inf))
+                score = lax.dot_general(query[k], kbuf[b * 8 + k], NT, preferred_element_type=f32) * HEAD ** (-0.5)
+                old.append(jnp.where(slot_index < limit[pl.ds(b * 8 + k, 1), :], score, -jnp.inf))
             old = jnp.concatenate(old, axis=0)
-            part = [pl.ds(pl.multiple_of(h * (PART - SIDE) + s * SIDE + g * 8, 8), 8) for s in range(STEPS)]
+            part = [pl.ds(pl.multiple_of(h * (PART - SIDE) + s * SIDE + b * 8, 8), 8) for s in range(STEPS)]
             keys = jnp.concatenate([nk[w, :] for w in part], axis=0).astype(bf16)
             values = jnp.concatenate([nv[w, :] for w in part], axis=0).astype(bf16)
-            new = lax.dot_general(jnp.concatenate(q, axis=0), keys, NT, preferred_element_type=f32) * HEAD ** (-0.5)
+            new = lax.dot_general(jnp.concatenate(query, axis=0), keys, NT, preferred_element_type=f32) * HEAD ** (-0.5)
             new = jnp.where(fresh, new, -jnp.inf)
             top = jnp.maximum(jnp.max(old, axis=-1, keepdims=True), jnp.max(new, axis=-1, keepdims=True))
             old = jnp.exp(old - top)
@@ -409,8 +432,8 @@
             fresh_part = jnp.dot(new, values, preferred_element_type=f32)
             for k in range(8):
                 rows = slice(k * 16, (k + 1) * 16)
-                ao[pl.ds(g * 8 + k, 16, stride=ROWS), :] = (
-                    jnp.dot(old[rows], vbuf[g * 8 + k], preferred_element_type=f32) + fresh_part[rows]
+                ao[pl.ds(b * 8 + k, 16, stride=ROWS), :] = (
+                    jnp.dot(old[rows], vbuf[b * 8 + k], preferred_element_type=f32) + fresh_part[rows]
                 )
             return carry
 
@@ -444,12 +467,6 @@
         att_ref(0, 0), att_ref(0, 1), hid_ref(0), hid_ref(1), att_ref(1, 0), att_ref(1, 1), out_ref(0), out_ref(1)
     ]
 
-    def g(step, n, own=None):
-        if step == 1:
-            g1(n, refs[n], own)
-        else:
-            (g2, g3, g4)[step - 2](n, refs[n])
-
     def first_out(h):
         hid[h, t] = project_out(0, h, resid[h * PART : (h + 1) * PART, :])
         g(1, 2 + h)
@@ -470,70 +487,70 @@
     start_exchange()
     prepare()
     pack_o(0)
-    o1(0)
+    pack_q(0)
+    q(1,0)
+    start_second()
+    pack_o(1)
     for copy in load_x:
         copy.wait()
     pick_own()
     normalize(0, 0, FLAT, lambda rows, j: xin[rows, j * CHUNK : (j + 1) * CHUNK])
-    pack_q(0)
-    q1(0)
-    start_second()
-    pack_o(1)
-    q2(0)
-    o2(0)
-    q3(0)
+    q(2,0)
+    q(3,0)
     pack_q(1)
-    q1(1)
-    o3(0)
-    q4(0)
-    q5(0)
-    project_in(0, 0, FLAT)
-    attend(0, 0)
-    g(1, 0)
-    attend(0, 1)
-    g(1, 1)
+    q(1,1)
+    o(1,0)
+    q(4,0)
+    q(5,0)
+    project_in(0,0,FLAT)
+    attend(0,0)
+    g(1,0)
+    o(2,0)
+    attend(0,1)
+    g(1,1)
     load_kv(1)
-    g(2, 0)
-    q2(1)
-    g(2, 1)
-    g(3, 0)
-    o4(0)
-    o5(0)
-    g(3, 1)
-    g(4, 0)
+    g(2,0)
+    g(2,1)
+    g(3,0)
+    o(3,0)
+    g(3,1)
+    q(2,1)
+    g(4,0)
+    o(4,0)
+    g(4,1)
+    o(5,0)
     first_out(0)
-    q3(1)
-    g(4, 1)
     first_out(1)
-    o1(1)
-    g(2, 2)
-    g(2, 3)
-    g(3, 2)
-    q4(1)
-    q5(1)
-    g(4, 2)
-    o2(1)
+    q(3,1)
+    g(2,2)
+    g(2,3)
+    o(1,1)
+    g(3,2)
+    g(3,3)
+    g(4,2)
+    q(4,1)
+    q(5,1)
     second_in(0)
-    g(3, 3)
-    g(4, 3)
+    o(2,1)
+    g(4,3)
     second_in(1)
-    g(2, 4)
-    g(2, 5)
-    g(3, 4)
-    o3(1)
-    o4(1)
-    g(3, 5)
-    o5(1)
-    g(4, 4)
+    g(2,4)
+    g(2,5)
+    o(3,1)
+    g(3,4)
+    g(3,5)
+    g(4,4)
+    o(4,1)
+    o(5,1)
     second_out(0)
-    g(4, 5)
+    g(4,5)
     second_out(1)
-    g(2, 6)
-    g(2, 7)
-    g(3, 6)
-    g(3, 7)
-    g(4, 6)
-    g(4, 7)
+    g(2,6)
+    g(2,7)
+    g(3,6)
+    g(3,7)
+    g(4,6)
+    g(4,7)
     for copy in keep:
         copy.wait()
     for copy in sent:
@@ -578,9 +595,9 @@
             pltpu.VMEM((ROWS, SLOTS), f32),
             dma((LAYERS, TP)), dma((LAYERS, TP)),
             dma((LAYERS,)), dma((LAYERS, 3)),
-            dma((LAYERS, 15)), dma((LAYERS, 15)),
             dma((LAYERS, 16)), dma((LAYERS, 16)),
-            dma((4 * PARTS, 7)), dma((4 * PARTS, 7)),
+            dma((LAYERS, 16)), dma((LAYERS, 16)),
+            dma((4 * PARTS, 8)), dma((4 * PARTS, 8)),
             dma((4 + PARTS * STEPS,)),
         ],
         compiler_params=pltpu.CompilerParams(

time: 188 us -> 181 us (0.963); the launches traced: 185 us -> 181 us
  Pallas kernels: 183 us -> 178 us
    pallas_call x1, Pallas kernels: 178 us -> 173 us  [fused(): pl.pallas_call(kernel, out_shape=jax.ShapeDtypeStruct((PARTS, TP, PART, C...]
where the time goes in v3:
time: 181 us
  Pallas kernels  178 us (98%)
    pallas_call x1, Pallas kernels, fused(): pl.pallas_call(kernel, out_shape=jax.ShapeDtypeStruct((PARTS, TP, PART, C...  173 us
    pallas_call x1, Pallas kernels, restore(): pl.pallas_call(restore_kernel, out_shape=jax.ShapeDtypeStruct((STEPS, ROW...  5.03 us

profile of v3, /device:TPU:32, one launch (start us, length us, event | category | flops | bytes accessed | tf_op | source)
XLA Modules:
  0.0 180.6 jit_solution(967405345116642578)
XLA Ops:
  0.0 0.6 maximum_bitcast_fusion.frequency
  0.6 173.2 %shard_map.91.hidden = bf16[2,8,128,640]{3,2,1,0:T(8,128)(2,1)} custom-call(bf16[4,64,5120]{2,1,0:T(8,128)(2,1)} %x_hbm.1, bf16[80,6144]{1,0:T(8,128)(2,1)} %bitcast.11, bf16[80,4096]{1,0:T(8,128)(2,1)} %bitcast.12, f32[2,5120]{1,0:T(2,128)} %gains.1, f32[2,1,128]{2,1,0:T(1,128)} %bitcast.13, f32[2,1,128]{2,1,0:T(1,128)} %bitcast.14, s32[1,64]{1,0:T(1,128)} %bitcast.15, ...), custom_call_target="tpu_custom_call" | custom-call | tf_op jit(solution)/shard_map/pallas_call | solution.py:568
  173.8 0.0 copy-start
  173.8 1.7 copy-done
  175.6 5.0 %shard_map.92 = bf16[4,64,5120]{2,1,0:T(8,128)(2,1)} custom-call(bf16[2,8,128,640]{3,2,1,0:T(8,128)(2,1)S(1)} %copy-done), custom_call_target="tpu_custom_call" | custom-call | tf_op jit(solution)/shard_map/pallas_call | solution.py:619
  (1 shorter events, 0.0 us)
Async XLA Ops:
  173.8 1.7 copy-start

commit v4 on v3

--- a/solution.py
+++ b/solution.py
@@ -489,13 +489,13 @@
     pack_o(0)
     pack_q(0)
     q(1,0)
-    start_second()
     pack_o(1)
     for copy in load_x:
         copy.wait()
-    pick_own()
     normalize(0, 0, FLAT, lambda rows, j: xin[rows, j * CHUNK : (j + 1) * CHUNK])
     q(2,0)
+    start_second()
+    pick_own()
     q(3,0)
     pack_q(1)
     q(1,1)
@@ -522,9 +522,9 @@
     first_out(0)
     first_out(1)
     q(3,1)
+    o(1,1)
     g(2,2)
     g(2,3)
-    o(1,1)
     g(3,2)
     g(3,3)
     g(4,2)

time: 181 us -> 175 us (0.967)
  Pallas kernels: 178 us -> 171 us
    pallas_call x1, Pallas kernels: 173 us -> 166 us  [fused(): pl.pallas_call(kernel, out_shape=jax.ShapeDtypeStruct((PARTS, TP, PART, C...]
where the time goes in v4:
time: 175 us; the launch traced here: 174 us
  Pallas kernels  171 us (98%)
    pallas_call x1, Pallas kernels, fused(): pl.pallas_call(kernel, out_shape=jax.ShapeDtypeStruct((PARTS, TP, PART, C...  166 us
    pallas_call x1, Pallas kernels, restore(): pl.pallas_call(restore_kernel, out_shape=jax.ShapeDtypeStruct((STEPS, ROW...  5.03 us

profile of v4, /device:TPU:32, one launch (start us, length us, event | category | flops | bytes accessed | tf_op | source)
XLA Modules:
  0.0 173.7 jit_solution(5854648385741560828)
XLA Ops:
  0.0 0.6 maximum_bitcast_fusion.frequency
  0.6 166.3 %shard_map.91.hidden = bf16[2,8,128,640]{3,2,1,0:T(8,128)(2,1)} custom-call(bf16[4,64,5120]{2,1,0:T(8,128)(2,1)} %x_hbm.1, bf16[80,6144]{1,0:T(8,128)(2,1)} %bitcast.11, bf16[80,4096]{1,0:T(8,128)(2,1)} %bitcast.12, f32[2,5120]{1,0:T(2,128)} %gains.1, f32[2,1,128]{2,1,0:T(1,128)} %bitcast.13, f32[2,1,128]{2,1,0:T(1,128)} %bitcast.14, s32[1,64]{1,0:T(1,128)} %bitcast.15, ...), custom_call_target="tpu_custom_call" | custom-call | tf_op jit(solution)/shard_map/pallas_call | solution.py:568
  166.9 0.0 copy-start
  167.0 1.7 copy-done
  168.7 5.0 %shard_map.92 = bf16[4,64,5120]{2,1,0:T(8,128)(2,1)} custom-call(bf16[2,8,128,640]{3,2,1,0:T(8,128)(2,1)S(1)} %copy-done), custom_call_target="tpu_custom_call" | custom-call | tf_op jit(solution)/shard_map/pallas_call | solution.py:619
  (1 shorter events, 0.0 us)
Async XLA Ops:
  166.9 1.7 %copy-start = (bf16[2,8,128,640]{3,2,1,0:T(8,128)(2,1)S(1)}, bf16[2,8,128,640]{3,2,1,0:T(8,128)(2,1)}, u32[]{:S(2)}) copy-start(bf16[2,8,128,640]{3,2,1,0:T(8,128)(2,1)} %shard_map.91.hidden) | copy-start | bytes 7864324

commit v5 on v4

--- a/solution.py
+++ b/solution.py
@@ -33,7 +33,7 @@
 bf16 = jnp.bfloat16
 
 O_Z_FIRST = (True, True)
-G_Z_FIRST = (True, False, True, False, True, False, True, False)
+G_Z_FIRST = (True, False, True, False, True, False, False, True)
 NT = (((1,), (1,)), ((), ()))
 
 

time: 175 us -> 173 us (0.989)
  Pallas kernels: 171 us -> 168 us
    pallas_call x1, Pallas kernels: 166 us -> 163 us  [fused(): pl.pallas_call(kernel, out_shape=jax.ShapeDtypeStruct((PARTS, TP, PART, C...]
where the time goes in v5:
time: 173 us; the launch traced here: 171 us
  Pallas kernels  168 us (97%)
  local copies, waits for them, and re-layouts  1.73 us (1%)
    pallas_call x1, Pallas kernels, fused(): pl.pallas_call(kernel, out_shape=jax.ShapeDtypeStruct((PARTS, TP, PART, C...  163 us
    pallas_call x1, Pallas kernels, restore(): pl.pallas_call(restore_kernel, out_shape=jax.ShapeDtypeStruct((STEPS, ROW...  5.03 us

profile of v5, /device:TPU:32, one launch (start us, length us, event | category | flops | bytes accessed | tf_op | source)
XLA Modules:
  0.0 170.7 jit_solution(6733823933867628725)
XLA Ops:
  0.0 0.6 maximum_bitcast_fusion.frequency
  0.6 163.3 %shard_map.91.hidden = bf16[2,8,128,640]{3,2,1,0:T(8,128)(2,1)} custom-call(bf16[4,64,5120]{2,1,0:T(8,128)(2,1)} %x_hbm.1, bf16[80,6144]{1,0:T(8,128)(2,1)} %bitcast.11, bf16[80,4096]{1,0:T(8,128)(2,1)} %bitcast.12, f32[2,5120]{1,0:T(2,128)} %gains.1, f32[2,1,128]{2,1,0:T(1,128)} %bitcast.13, f32[2,1,128]{2,1,0:T(1,128)} %bitcast.14, s32[1,64]{1,0:T(1,128)} %bitcast.15, ...), custom_call_target="tpu_custom_call" | custom-call | tf_op jit(solution)/shard_map/pallas_call | solution.py:568
  163.9 0.0 copy-start
  163.9 1.7 %copy-done = bf16[2,8,128,640]{3,2,1,0:T(8,128)(2,1)S(1)} copy-done((bf16[2,8,128,640]{3,2,1,0:T(8,128)(2,1)S(1)}, bf16[2,8,128,640]{3,2,1,0:T(8,128)(2,1)}, u32[]{:S(2)}) %copy-start) | copy-done | bytes 2621464
  165.7 5.0 %shard_map.92 = bf16[4,64,5120]{2,1,0:T(8,128)(2,1)} custom-call(bf16[2,8,128,640]{3,2,1,0:T(8,128)(2,1)S(1)} %copy-done), custom_call_target="tpu_custom_call" | custom-call | tf_op jit(solution)/shard_map/pallas_call | solution.py:619
  (1 shorter events, 0.0 us)
Async XLA Ops:
  163.9 1.7 %copy-start = (bf16[2,8,128,640]{3,2,1,0:T(8,128)(2,1)S(1)}, bf16[2,8,128,640]{3,2,1,0:T(8,128)(2,1)}, u32[]{:S(2)}) copy-start(bf16[2,8,128,640]{3,2,1,0:T(8,128)(2,1)} %shard_map.91.hidden) | copy-start | bytes 7864324
